TPU v7x, 32 devices: a whole 2x2x4 slice. The times are simulated.
32 devices in a mesh: role: 2 (over y), dev: 16 (over z, x, core).
Axes of the slice: x: 2, y: 2, z: 4, core: 2. Of those that a mesh axis runs over, the one named last changes fastest.
Arguments:
- features: bfloat16 [2, 32, 32, 64, 128], P('role', None, 'dev'), may hold values from -6 to 6
- labels: bfloat16 [2, 32, 64, 128], P('role', 'dev'), may hold values from 0 to 1
- crop_block: int32 [2, 16, 16], P('role'), may hold values from -1 to 15, as said below
- weight: float32 [64, 864], P('dev'), may hold values from -0.21875 to 0.21875
- gain: float32 [64], P('dev'), may hold values from 0.1 to 1.9
- shift: float32 [64], P('dev'), may hold values from -3 to 3
- head: float32 [64], P('dev'), may hold values from -1.5 to 1.5
- run_mean: float32 [64], P('dev'), may hold values from -2 to 2
- run_var: float32 [64], P('dev'), may hold values from 0.5 to 2
Outputs:
- scores: float32 [2, 32, 64, 128], P('role', 'dev')
- weight_grad: float32 [64, 864], P('dev')
- vector_grad: float32 [64, 3], P('dev')
Inputs may be any that keep to these rules, and one draw needn't show every extreme that they name: crop_block[g, s, t] >= 0 is the row block b that source s of group g sends to learner t; -1 means no crop. Source s always sends to learner s, and to between 4 and 12 learners in all.
All inputs are finite; a program needn't handle non-finite values.
Results may differ from a plain program's by a relative error of at most 0.002.
The roundings to bfloat16 on the way count: a program that leaves them out, or rounds other values in their place, can miss the bound.
Values may be sent and summed in bfloat16 or wider, within the bound.
A program may use at most 128 MiB of HBM per device.

v0:
```python
import jax
import jax.numpy as jnp
from jax import lax
from jax.sharding import PartitionSpec as P

CY = 4


epsilon = 1e-05


def extended(cells, sides, width):
    for axis, dim in sides:
        count = lax.axis_size(axis)
        ends = count - 1
        head = lax.slice_in_dim(cells, 0, width, axis=dim)
        tail = lax.slice_in_dim(cells, cells.shape[dim] - width, cells.shape[dim], axis=dim)
        cells = jnp.concatenate(
            [
                lax.ppermute(tail, axis, [(i, (i + 1) % count) for i in range(ends)]),
                cells,
                lax.ppermute(head, axis, [((i + 1) % count, i) for i in range(ends)]),
            ],
            axis=dim,
        )
    return cells


def column_shift(values, offset):
    if offset < 0:
        return jnp.pad(values[..., :-1], [(0, 0)] * (values.ndim - 1) + [(1, 0)])
    return jnp.pad(values[..., 1:], [(0, 0)] * (values.ndim - 1) + [(0, 1)])


def plane_patches(padded, planes, height):
    shifted = [
        padded[:, shift_z : shift_z + planes, :, shift_y : shift_y + height, :]
        for shift_z in range(3)
        for shift_y in range(3)
    ]
    return jnp.stack(shifted, 0).reshape(9 * padded.shape[0], -1)


def conv_taps(padded, weight_taps, planes, height):
    columns = padded.shape[-1]
    patches = plane_patches(padded, planes, height)
    outputs = [
        jnp.dot(weight_taps[tap], patches, preferred_element_type=jnp.float32).reshape(
            weight_taps.shape[1], -1, columns
        )
        for tap in range(3)
    ]
    summed = outputs[1] + column_shift(outputs[0], -1) + column_shift(outputs[2], 1)
    return summed.reshape(weight_taps.shape[1], -1)


def local_total(members):
    return tuple(
        (jnp.broadcast_to(jnp.sum(member, 1, keepdims=True), member.shape) for member in members)
    )


def learn(
    crop_data,
    targets,
    live_flags,
    cell_counts,
    weight_taps,
    gain_value,
    shift_value,
    head_value,
    combine,
):
    slot_group = 8
    channels, planes, slots, crop_rows, columns = crop_data.shape
    out_channels = weight_taps.shape[1]
    row_cells = crop_rows * columns
    targets = targets.reshape(planes, slots, row_cells).astype(jnp.float32)
    live_weights = live_flags.astype(jnp.float32)
    groups = slots // slot_group

    def select_group(array, crop_position, axis):
        return lax.dynamic_slice_in_dim(array, crop_position, slot_group, axis)

    def update_group(array, values, crop_position, axis):
        return lax.dynamic_update_slice_in_dim(array, values, crop_position, axis)

    def crop_patches(crop_position):
        group_block = select_group(crop_data, crop_position, 2)
        return jnp.pad(group_block, ((0, 0), (1, 1), (0, 0), (1, 1), (0, 0)))

    def forward(number, stored):
        crop_position = number * slot_group
        conv_out = conv_taps(crop_patches(crop_position), weight_taps, planes, crop_rows)
        conv_out = conv_out.reshape(out_channels, planes, slot_group, row_cells).astype(
            jnp.bfloat16
        )
        return update_group(stored, conv_out, crop_position, 2)

    stored = lax.fori_loop(
        0, groups, forward, jnp.zeros((out_channels, planes, slots, row_cells), jnp.bfloat16)
    )
    slot_sums = jnp.einsum(
        "cpsk,k->cs",
        stored,
        jnp.ones((row_cells,), jnp.bfloat16),
        preferred_element_type=jnp.float32,
    )
    (mean_sum,) = combine((slot_sums,))
    channel_means = mean_sum / cell_counts[None, :]

    def centred(number, squares):
        crop_position = number * slot_group
        diff = (
            select_group(stored, crop_position, 2).astype(jnp.float32)
            - select_group(channel_means, crop_position, 1)[:, None, :, None]
        ) * select_group(live_weights, crop_position, 0)[None, None, :, None]
        return update_group(squares, jnp.sum(diff * diff, (1, 3)), crop_position, 1)

    empty_statistics = jnp.zeros((out_channels, slots), jnp.float32)
    squares = lax.fori_loop(0, groups, centred, empty_statistics)
    (square_sum,) = combine((squares,))
    inverse_std = lax.rsqrt(square_sum / cell_counts[None, :] + epsilon)

    def local_grads(crop_position):
        normal = (
            select_group(stored, crop_position, 2).astype(jnp.float32)
            - select_group(channel_means, crop_position, 1)[:, None, :, None]
        ) * select_group(inverse_std, crop_position, 1)[:, None, :, None]
        before = gain_value[:, None, None, None] * normal + shift_value[:, None, None, None]
        hidden = jax.nn.relu(before)
        ranked_crops = jnp.einsum(
            "cpsk,c->psk", hidden, head_value, precision=lax.Precision.HIGHEST
        )
        residual = (
            select_group(live_weights, crop_position, 0)[None, :, None]
            * (ranked_crops - select_group(targets, crop_position, 1))
            / select_group(cell_counts, crop_position, 0)[None, :, None]
        )
        dbefore = jnp.where(before > 0, head_value[:, None, None, None] * residual[None], 0.0)
        return (normal, hidden, residual, dbefore)

    def backward_sums(number, running):
        first_sums, second_sums, vector_sums = running
        crop_position = number * slot_group
        normal, hidden, residual, dbefore = local_grads(crop_position)
        dnormal = dbefore * gain_value[:, None, None, None]
        first_sums = update_group(first_sums, jnp.sum(dnormal, (1, 3)), crop_position, 1)
        second_sums = update_group(second_sums, jnp.sum(dnormal * normal, (1, 3)), crop_position, 1)
        vector_terms = jnp.stack(
            [
                jnp.sum(dbefore * normal, (1, 2, 3)),
                jnp.sum(dbefore, (1, 2, 3)),
                jnp.sum(hidden * residual[None], (1, 2, 3)),
            ],
            1,
        )
        return (first_sums, second_sums, vector_sums + vector_terms)

    first_sums, second_sums, vector_grad = lax.fori_loop(
        0,
        groups,
        backward_sums,
        (empty_statistics, empty_statistics, jnp.zeros((out_channels, 3), jnp.float32)),
    )
    first_total, second_total = combine((first_sums, second_sums))
    first_mean = first_total / cell_counts[None, :]
    second_mean = second_total / cell_counts[None, :]

    def weight_step(number, summed):
        crop_position = number * slot_group
        normal, hidden, residual, dbefore = local_grads(crop_position)
        dnormal = dbefore * gain_value[:, None, None, None]
        dfield = (
            select_group(live_weights, crop_position, 0)[None, None, :, None]
            * select_group(inverse_std, crop_position, 1)[:, None, :, None]
            * (
                dnormal
                - select_group(first_mean, crop_position, 1)[:, None, :, None]
                - normal * select_group(second_mean, crop_position, 1)[:, None, :, None]
            )
        )
        dfield = dfield.astype(jnp.bfloat16).reshape(out_channels, -1, columns)
        patches = plane_patches(crop_patches(crop_position), planes, crop_rows)
        moved = [column_shift(dfield, 1), dfield, column_shift(dfield, -1)]
        pieces = [
            lax.dot_general(
                part.reshape(out_channels, -1),
                patches,
                (((1,), (1,)), ((), ())),
                preferred_element_type=jnp.float32,
            )
            for part in moved
        ]
        return summed + jnp.stack(pieces, 0)

    tap_grad = lax.fori_loop(
        0, groups, weight_step, jnp.zeros((3, out_channels, 9 * channels), jnp.float32)
    )
    weight_grad = (
        tap_grad.reshape(3, out_channels, 9, channels)
        .transpose(1, 2, 0, 3)
        .reshape(out_channels, 27 * channels)
    )
    return (weight_grad, vector_grad)


def per_device(features, labels, crop_block, weight, gain, shift, head, run_mean, run_var):
    vectors = jnp.stack([gain, shift, head, run_mean, run_var], 1).astype(jnp.bfloat16)
    weight_b, vectors_b = (
        lax.all_gather(weight.astype(jnp.bfloat16), "dev", axis=0, tiled=True),
        lax.all_gather(vectors, "dev", axis=0, tiled=True),
    )
    vector_f = vectors_b.astype(jnp.float32)
    gain_value = vector_f[:, 0]
    shift_value = vector_f[:, 1]
    head_value = vector_f[:, 2]
    mean_value = vector_f[:, 3]
    spread_value = vector_f[:, 4]
    out_channels = weight_b.shape[0]
    own_slab = features[0]
    channels, planes, height, columns = own_slab.shape
    weight_taps = (
        weight_b.reshape(out_channels, 9, 3, channels)
        .transpose(2, 0, 1, 3)
        .reshape(3, out_channels, 9 * channels)
    )
    bordered = extended(own_slab, (("dev", 1),), 1)
    padded = jnp.pad(bordered, ((0, 0), (0, 0), (1, 1), (0, 0)))
    inverse_std = lax.rsqrt(spread_value + epsilon)
    plane_scores = []
    for plane_index in range(planes):
        conv_out = conv_taps(padded[:, plane_index : plane_index + 3, None], weight_taps, 1, height)
        hidden = jax.nn.relu(
            gain_value[:, None] * (conv_out - mean_value[:, None]) * inverse_std[:, None]
            + shift_value[:, None]
        )
        plane_scores.append(
            jnp.dot(head_value, hidden, precision=lax.Precision.HIGHEST).reshape(height, columns)
        )
    scores = jnp.stack(plane_scores)[None]
    route_table = crop_block[0]
    slots = route_table.shape[0]
    own_index = lax.axis_index("dev")
    block_count = height // CY
    crop_cells = planes * CY * columns
    row_entries = lax.dynamic_slice_in_dim(route_table, own_index, 1, 0)[0]
    col_entries = lax.dynamic_slice_in_dim(route_table, own_index, 1, 1)[:, 0]
    send_live = row_entries >= 0
    chosen = jnp.maximum(row_entries, 0)
    slab_blocks = own_slab.reshape(channels, planes, block_count, CY, columns)
    send_crops = jnp.take(slab_blocks, chosen, axis=2)
    send_crops = jnp.where(
        send_live[None, None, :, None, None], send_crops, jnp.zeros((), jnp.bfloat16)
    )
    label_blocks = labels[0].reshape(1, planes, block_count, CY, columns)
    send_labels = jnp.take(label_blocks, chosen, axis=2)
    send_labels = jnp.where(
        send_live[None, None, :, None, None], send_labels, jnp.zeros((), jnp.bfloat16)
    )
    crop_data, crop_labels = (
        lax.all_to_all(send_crops, "dev", split_axis=2, concat_axis=2, tiled=True),
        lax.all_to_all(send_labels, "dev", split_axis=2, concat_axis=2, tiled=True),
    )
    live_flags = col_entries >= 0
    cell_counts = jnp.broadcast_to(jnp.sum(live_flags.astype(jnp.float32)), (slots,)) * crop_cells
    weight_terms, vector_terms = learn(
        crop_data,
        crop_labels[0],
        live_flags,
        cell_counts,
        weight_taps,
        gain_value,
        shift_value,
        head_value,
        local_total,
    )
    weight_all, vector_all = lax.psum((weight_terms, vector_terms), ("role", "dev"))
    row_share = weight_all.shape[0] // lax.axis_size("dev")
    row_start = own_index * row_share
    weight_grad = lax.dynamic_slice_in_dim(weight_all, row_start, row_share, 0)
    vector_grad = lax.dynamic_slice_in_dim(vector_all, row_start, row_share, 0)
    return (scores, weight_grad, vector_grad)


def solution(mesh):
    in_specs = (
        P("role", None, "dev", None, None),
        P("role", "dev", None, None),
        P("role", None, None),
        P("dev", None),
        P("dev"),
        P("dev"),
        P("dev"),
        P("dev"),
        P("dev"),
    )
    out_specs = (P("role", "dev", None, None), P("dev", None), P("dev", None))
    return jax.shard_map(
        per_device, mesh=mesh, in_specs=in_specs, out_specs=out_specs, check_vma=False
    )
```

profile of v0, /device:TPU:0, one launch (start us, length us, event | category | flops | bytes accessed | tf_op | source)
XLA Modules:
  0.0 446.8 jit_solution(17175542991375096338)
XLA Ops:
  7.3 2.4 fusion.149
  9.7 3.2 collective-permute-start
  15.5 8.5 %all-to-all-start.1 = ((bf16[1,2,16,4,128]{4,3,1,0,2:T(4,128)(2,1)}), bf16[1,2,16,4,128]{4,3,1,0,2:T(4,128)(2,1)S(1)}, u32[]{:S(2)}, u32[]{:S(2)}) async-start(bf16[1,2,16,4,128]{4,3,1,0,2:T(4,128)(2,1)} %fusion.140), calls=%async_computation.1 | async-start | bytes 65536 | tf_op jit(solution)/shard_map/all_to_all | solution.py:263
  24.0 22.0 %all-gather.1 = bf16[16,4,864]{2,1,0:T(4,128)(2,1)S(1)} all-gather(bf16[1,4,864]{2,1,0:T(4,128)(2,1)S(1)} %convert_bitcast_fusion), channel_id=1, replica_groups=mesh['role'=2,'dev'=16] {'dev'}, dimensions={0}, use_global_device_ids=true | all-gather | bytes 117504 | tf_op jit(solution)/shard_map/all_gather | solution.py:211
  48.0 17.4 %all-gather = bf16[16,4,5]{2,1,0:T(4,128)(2,1)S(1)} all-gather(bf16[1,4,5]{2,1,0:T(4,128)(2,1)S(1)} %bitcast.606), channel_id=1, replica_groups=mesh['role'=2,'dev'=16] {'dev'}, dimensions={0}, use_global_device_ids=true | all-gather | bytes 680 | tf_op jit(solution)/shard_map/all_gather | solution.py:212
  66.7 1.7 gather_fusion
  68.4 2.5 select_bitcast_fusion
  73.9 3.7 all-to-all-start
  78.3 2.3 fusion.84
  84.4 2.8 fusion.118
  87.2 2.8 fusion.115
  90.0 2.8 fusion.109
  92.8 3.3 fusion.106
  96.1 2.8 fusion.112
  98.9 2.8 fusion.103
  106.0 2.9 fusion.96
  108.9 3.9 fusion.95
  115.9 66.7 %while.62 = (s32[]{:T(128)}, bf16[64,2,16,512]{3,2,1,0:T(8,128)(2,1)S(1)}, bf16[32,2,16,4,128]{4,3,2,1,0:T(4,128)(2,1)S(1)}, bf16[3,64,288]{2,1,0:T(8,128)(2,1)S...) while((s32[]{:T(128)}, bf16[64,2,16,512]{3,2,1,0:T(8,128)(2,1)S(1)}, ...), condition=%wide.region_1.2_spmd, body=%wide.region_0.1_spmd.sunk | while | flops 907542528 | bytes 87638184 | solution.py:100
  125.9 8.8 %reshape.304 = bf16[288,8192]{1,0:T(8,128)(2,1)} reshape(bf16[9,32,2,8,4,128]{5,4,3,2,1,0:T(4,128)(2,1)} %fusion.219) | data formatting | bytes 9437184 | tf_op jit(solution)/shard_map/while/body/eval_jaxpr/reshape | solution.py:41
  134.8 3.5 convolution_bitcast_fusion.13
  145.4 2.5 convert_element_type.155
  159.3 8.8 %reshape.304 = bf16[288,8192]{1,0:T(8,128)(2,1)} reshape(bf16[9,32,2,8,4,128]{5,4,3,2,1,0:T(4,128)(2,1)} %fusion.219) | data formatting | bytes 9437184 | tf_op jit(solution)/shard_map/while/body/eval_jaxpr/reshape | solution.py:41
  168.2 3.5 convolution_bitcast_fusion.13
  177.1 1.6 fusion.220
  178.7 2.5 convert_element_type.155
  185.2 4.9 %while.63 = (s32[]{:T(128)}, f32[64,16]{1,0:T(8,128)S(1)}, bf16[64,2,16,512]{3,2,1,0:T(8,128)(2,1)S(1)}, f32[64,16]{1,0:T(8,128)}, f32[16]{0:T(128)}, /*index=5*/s32[]{:T(128)}, s32[]{:T(128)}, s32[]{:T(128)}, s32[]{:T(128)}) while((s32[]{:T(128)}, f32[64,16]{1,0:T(8,128)S(1)}, bf16[64,2,16,512]{3,2,1,0:T(8,128)(2,1)S(1)}, ...), condition=%wide.region_7.8_spmd, body=%wide.region_5.7_spmd.sunk | while | flops 2620934 | bytes 1061115 | solution.py:121
  192.1 28.1 %while.64 = (s32[]{:T(128)}, f32[64,16]{1,0:T(8,128)}, f32[64,16]{1,0:T(8,128)}, f32[64,3]{0,1:T(4,128)}, f32[64,1]{0,1:T(1,128)S(1)}, /*index=5*/bf16[64,2,16,5...) while((s32[]{:T(128)}, f32[64,16]{1,0:T(8,128)}, ...), condition=%wide.region_15.16_spmd.clone, body=%wide.region_9.15_spmd.clone.sunk | while | flops 18898500 | bytes 6493121 | solution.py:160
  193.5 3.0 fusion.224
  198.8 3.2 multiply_reduce_fusion.7
  207.4 3.0 fusion.224
  212.8 3.2 multiply_reduce_fusion.7
  223.3 85.9 %while.65 = (s32[]{:T(128)}, f32[3,64,288]{2,1,0:T(8,128)S(1)}, f32[16]{0:T(128)}, f32[64,16]{0,1:T(8,128)S(1)}, f32[64,1]{0,1:T(1,128)S(1)}, /*index=5*/bf16[64...) while((s32[]{:T(128)}, f32[3,64,288]{2,1,0:T(8,128)S(1)}, ...), condition=%wide.region_19.20_spmd.clone, body=%wide.region_18.19_spmd.clone.sunk | while | flops 922993152 | bytes 84928640 | solution.py:197
  233.7 8.8 %reshape.305 = bf16[288,8192]{1,0:T(8,128)(2,1)} reshape(bf16[9,32,2,8,4,128]{5,4,3,2,1,0:T(4,128)(2,1)} %fusion.241) | data formatting | bytes 9437184 | tf_op jit(solution)/shard_map/while/body/eval_jaxpr/reshape | solution.py:41
  244.8 3.0 fusion.243
  250.3 2.6 multiply_convert_fusion.2
  252.9 1.7 reshape.306
  255.4 4.2 convolution_bitcast_fusion.17
  260.0 2.3 convolution_bitcast_fusion.15
  263.0 2.3 convolution_bitcast_fusion.16
  276.6 8.8 %reshape.305 = bf16[288,8192]{1,0:T(8,128)(2,1)} reshape(bf16[9,32,2,8,4,128]{5,4,3,2,1,0:T(4,128)(2,1)} %fusion.241) | data formatting | bytes 9437184 | tf_op jit(solution)/shard_map/while/body/eval_jaxpr/reshape | solution.py:41
  287.6 3.0 fusion.243
  293.2 2.6 multiply_convert_fusion.2
  295.7 1.7 reshape.306
  298.3 4.2 convolution_bitcast_fusion.17
  302.9 2.3 convolution_bitcast_fusion.15
  305.9 2.3 convolution_bitcast_fusion.16
  311.0 40.8 %psum.15 = f32[64,3]{1,0:T(8,128)S(1)} all-reduce(f32[64,3]{1,0:T(8,128)S(1)} %copy.145), channel_id=1, replica_groups=mesh['role'=2,'dev'=16] {'role','dev'}, use_global_device_ids=true, to_apply=%region_21.22 | all-reduce | flops 192 | bytes 1536 | tf_op jit(solution)/shard_map/psum | solution.py:278
  352.5 85.1 %all-reduce.13.cloned.1.call-done = f32[64,864]{0,1:T(8,128)} async-done(((f32[64,864]{0,1:T(8,128)}), f32[64,864]{0,1:T(8,128)}) %all-reduce.13.cloned.1.call-update) | async-done | bytes 221200 | tf_op jit(solution)/shard_map/psum | solution.py:278
  (257 shorter events, 123.2 us)
Async XLA Ops:
  7.2 7.0 %copy-start = (bf16[1,2,64,128]{3,2,1,0:T(8,128)(2,1)S(1)}, bf16[1,2,64,128]{3,2,1,0:T(8,128)(2,1)}, u32[]{:S(2)}) copy-start(bf16[1,2,64,128]{3,2,1,0:T(8,128)(2,1)} %param.18) | copy-start | bytes 98308
  7.2 6.9 %copy-start.12 = (s32[1,16,16]{2,1,0:T(8,128)S(1)}, s32[1,16,16]{2,1,0:T(8,128)}, u32[]{:S(2)}) copy-start(s32[1,16,16]{2,1,0:T(8,128)} %param.19) | copy-start | bytes 3076
  7.2 16.8 %copy-start.11 = (f32[4,864]{1,0:T(4,128)S(1)}, f32[4,864]{1,0:T(4,128)}, u32[]{:S(2)}) copy-start(f32[4,864]{1,0:T(4,128)} %param.20) | copy-start | bytes 41476
  7.2 40.6 %copy-start.17 = (f32[4]{0:T(128)S(1)}, f32[4]{0:T(128)}, u32[]{:S(2)}) copy-start(f32[4]{0:T(128)} %param.21) | copy-start | bytes 52
  7.2 40.6 %copy-start.13 = (f32[4]{0:T(128)S(1)}, f32[4]{0:T(128)}, u32[]{:S(2)}) copy-start(f32[4]{0:T(128)} %param.25) | copy-start | bytes 52
  7.2 40.6 %copy-start.14 = (f32[4]{0:T(128)S(1)}, f32[4]{0:T(128)}, u32[]{:S(2)}) copy-start(f32[4]{0:T(128)} %param.24) | copy-start | bytes 52
  7.2 40.6 %copy-start.15 = (f32[4]{0:T(128)S(1)}, f32[4]{0:T(128)}, u32[]{:S(2)}) copy-start(f32[4]{0:T(128)} %param.23) | copy-start | bytes 52
  7.2 40.6 %copy-start.16 = (f32[4]{0:T(128)S(1)}, f32[4]{0:T(128)}, u32[]{:S(2)}) copy-start(f32[4]{0:T(128)} %param.22) | copy-start | bytes 52
  7.3 58.8 %copy-start.7 = (bf16[1,32,2,64,128]{4,3,2,1,0:T(8,128)(2,1)S(1)}, bf16[1,32,2,64,128]{4,3,2,1,0:T(8,128)(2,1)}, u32[]{:S(2)}) copy-start(bf16[1,32,2,64,128]{4,3,2,1,0:T(8,128)(2,1)} %param.17) | copy-start | bytes 3145732
  9.7 68.6 %collective-permute-start = (bf16[32,1,64,128]{3,2,1,0:T(8,128)(2,1)}, bf16[32,1,64,128]{3,2,1,0:T(8,128)(2,1)}, u32[]{:S(2)}, u32[]{:S(2)}) collective-permute-start(bf16[32,1,64,128]{3,2,1,0:T(8,128)(2,1)} %get-tuple-element.1103), channel_id=1, source_target_pairs={{0,1},{1,2},{2,3},{3,4},{4,5},{5,6},{6,7},{7,8},{8,9},{9,10},{10,1... | collective-permute-start | bytes 1572872 | tf_op jit(solution)/shard_map/ppermute | solution.py:20
  12.8 65.4 %collective-permute-start.1 = (bf16[32,1,64,128]{3,2,1,0:T(8,128)(2,1)}, bf16[32,1,64,128]{3,2,1,0:T(8,128)(2,1)}, u32[]{:S(2)}, u32[]{:S(2)}) collective-permute-start(bf16[32,1,64,128]{3,2,1,0:T(8,128)(2,1)} %get-tuple-element.1104), channel_id=1, source_target_pairs={{1,0},{2,1},{3,2},{4,3},{5,4},{6,5},{7,6},{8,7},{9,8},{10,9},{11,1... | collective-permute-start | bytes 1572872 | tf_op jit(solution)/shard_map/ppermute | solution.py:22
  15.5 58.3 %all-to-all-start.1 = ((bf16[1,2,16,4,128]{4,3,1,0,2:T(4,128)(2,1)}), bf16[1,2,16,4,128]{4,3,1,0,2:T(4,128)(2,1)S(1)}, u32[]{:S(2)}, u32[]{:S(2)}) async-start(bf16[1,2,16,4,128]{4,3,1,0,2:T(4,128)(2,1)} %fusion.140), calls=%async_computation.1 | async-start | bytes 65536 | tf_op jit(solution)/shard_map/all_to_all | solution.py:263
  68.4 3.4 copy-start.8
  73.9 41.2 %all-to-all-start = ((bf16[32,2,16,4,128]{4,0,3,1,2:T(8,128)(2,1)}), bf16[32,2,16,4,128]{4,0,3,1,2:T(8,128)(2,1)S(1)}, u32[]{:S(2)}, u32[]{:S(2)}) async-start(bf16[32,2,16,4,128]{4,0,3,1,2:T(8,128)(2,1)} %select_bitcast_fusion), calls=%async_computation | async-start | bytes 2097152 | tf_op jit(solution)/shard_map/all_to_all | solution.py:262
  77.5 360.1 %all-reduce.13.cloned.1.call-start = ((), (), s32[]{:S(2)}) async-start(), calls=%async_computation.2 | async-start | bytes 884736 | tf_op jit(solution)/shard_map/psum | solution.py:278
  138.3 2.3 copy-start.2
  171.6 2.3 copy-start.2
  185.2 6.9 %copy-start.9 = (f32[64,1]{0,1:T(1,128)S(1)}, f32[64,1]{0,1:T(1,128)}, u32[]{:S(2)}) copy-start(f32[64,1]{0,1:T(1,128)} %get-tuple-element.1492) | copy-start | bytes 772
  185.2 6.9 %copy-start.10 = (f32[64,1]{0,1:T(1,128)S(1)}, f32[64,1]{0,1:T(1,128)}, u32[]{:S(2)}) copy-start(f32[64,1]{0,1:T(1,128)} %get-tuple-element.1489) | copy-start | bytes 772
  192.0 31.3 %copy-start.6 = (f32[3,64,288]{2,1,0:T(8,128)S(1)}, f32[3,64,288]{2,1,0:T(8,128)}, u32[]{:S(2)}) copy-start(f32[3,64,288]{2,1,0:T(8,128)} %custom-call.1) | copy-start | bytes 663556
  223.5 4.7 %copy-start.4 = (bf16[32,2,16,4,128]{4,3,2,1,0:T(4,128)(2,1)}, bf16[32,2,16,4,128]{4,3,2,1,0:T(4,128)(2,1)S(1)}, u32[]{:S(2)}) copy-start(bf16[32,2,16,4,128]{4,3,2,1,0:T(4,128)(2,1)S(1)} %get-tuple-element.1539) | copy-start | bytes 3145732 | tf_op jit(solution)/shard_map/while
  255.1 4.9 %slice-start = ((s8[4718592]{0:T(1024)(128)(4,1)}), s8[4194304]{0:T(1024)(128)(4,1)S(1)}, s32[]{:S(2)}) async-start(s8[4718592]{0:T(1024)(128)(4,1)} %bitcast.558), calls=%async_computation.3 | async-start | bytes 8388608 | tf_op jit(solution)/shard_map/while
  255.4 4.6 %slice-start.1 = ((s8[4718592]{0:T(1024)(128)(4,1)}), s8[524288]{0:T(1024)(128)(4,1)S(1)}, s32[]{:S(2)}) async-start(s8[4718592]{0:T(1024)(128)(4,1)} %bitcast.558), calls=%async_computation.4 | async-start | bytes 1048576 | tf_op jit(solution)/shard_map/while
  260.0 2.3 copy-start.3
  263.0 3.4 copy-start.5
  266.4 4.7 %copy-start.4 = (bf16[32,2,16,4,128]{4,3,2,1,0:T(4,128)(2,1)}, bf16[32,2,16,4,128]{4,3,2,1,0:T(4,128)(2,1)S(1)}, u32[]{:S(2)}) copy-start(bf16[32,2,16,4,128]{4,3,2,1,0:T(4,128)(2,1)S(1)} %get-tuple-element.1539) | copy-start | bytes 3145732 | tf_op jit(solution)/shard_map/while
  298.0 4.9 %slice-start = ((s8[4718592]{0:T(1024)(128)(4,1)}), s8[4194304]{0:T(1024)(128)(4,1)S(1)}, s32[]{:S(2)}) async-start(s8[4718592]{0:T(1024)(128)(4,1)} %bitcast.558), calls=%async_computation.3 | async-start | bytes 8388608 | tf_op jit(solution)/shard_map/while
  298.3 4.6 %slice-start.1 = ((s8[4718592]{0:T(1024)(128)(4,1)}), s8[524288]{0:T(1024)(128)(4,1)S(1)}, s32[]{:S(2)}) async-start(s8[4718592]{0:T(1024)(128)(4,1)} %bitcast.558), calls=%async_computation.4 | async-start | bytes 1048576 | tf_op jit(solution)/shard_map/while
  302.9 2.3 copy-start.3
  305.8 3.4 copy-start.5
  309.2 130.3 %copy-start.1 = (bf16[1,2,64,128]{3,2,1,0:T(8,128)(2,1)S(1)}, bf16[1,2,64,128]{3,2,1,0:T(8,128)(2,1)}, u32[]{:S(2)}) copy-start(bf16[1,2,64,128]{3,2,1,0:T(8,128)(2,1)} %param.18) | copy-start | bytes 98308
Sparse Core Ops, SparseCore 0:
  310.4 127.1 all-reduce.12
where the time goes:
time: 454 us; the launch traced here: 447 us
  local copies, waits for them, and re-layouts  143 us (31%)
  waiting for transfers between devices  85.2 us (19%)
  blocking collectives  80.3 us (18%)
  matrix products  61.6 us (14%)
  other arithmetic  43.3 us (10%)
  starting transfers between devices  16.6 us (4%)
  between operations  15.7 us (3%)
    psum x1, waiting for transfers between devices, per_device(): lax.psum((weight_terms, vector_terms), ('role', 'dev'))  85.1 us
    while x64, local copies, waits for them, and re-layouts  41.2 us
    psum x1, blocking collectives, per_device(): lax.psum((weight_terms, vector_terms), ('role', 'dev'))  40.8 us
    reshape x4, local copies, waits for them, and re-layouts, plane_patches(): return jnp.stack(shifted, 0).reshape(9 * padded.shape[0], -1)  35.3 us
    dot_general x12, matrix products, conv_taps(): jnp.dot(weight_taps[tap], patches, preferred_element_type=jnp.float32)  28.9 us
    all_gather x1, blocking collectives, per_device(): lax.all_gather(weight.astype(jnp.bfloat16), 'dev', axis=0, tiled=True)  22 us
    dot_general x6, matrix products, weight_step(): lax.dot_general(part.reshape(out_channels, -1), patches, (((1,), (1,)), (...  17.7 us
    all_gather x1, blocking collectives, per_device(): lax.all_gather(vectors, 'dev', axis=0, tiled=True)  17.4 us
  transfers between devices with their start and end apart: 5, of which 1 were waited for; matrix products, arithmetic and copies ran while one was open for 11% of the time, Pallas kernels for 0%

commit v1 on v0

v1 whole, which is shorter than its diff:
```python
import functools

import jax
import jax.numpy as jnp
from jax import lax
from jax.experimental import pallas as pl
from jax.experimental.pallas import tpu as pltpu
from jax.sharding import PartitionSpec as P

CY = 4
EPS = 1e-05
LANES = 128
F32 = jnp.float32
BF16 = jnp.bfloat16


def shift_lanes(value, offset):
    lane = lax.broadcasted_iota(jnp.int32, value.shape, 1)
    width = value.shape[1]
    if offset < 0:
        return jnp.where(lane == 0, 0.0, pltpu.roll(value, 1, 1))
    return jnp.where(lane == width - 1, 0.0, pltpu.roll(value, width - 1, 1))


def column(table, index):
    lane = lax.broadcasted_iota(jnp.int32, table.shape, 1)
    return jnp.sum(jnp.where(lane == index, table, 0.0), axis=1, keepdims=True)


def put_column(ref, rows, index, value):
    part = ref[rows, :]
    lane = lax.broadcasted_iota(jnp.int32, part.shape, 1)
    ref[rows, :] = jnp.where(lane == index, value, part)


def crop_tiles(planes, block, channels):
    for z in range(planes):
        for y in range(CY):
            cell_row = z * CY + y
            for dz in range(3):
                for dy in range(3):
                    zs, ys = z + dz - 1, y + dy - 1
                    if 0 <= zs < planes and 0 <= ys < CY:
                        yield (dz * 3 + dy) * channels, cell_row, zs, ys


def fill_patches(patch_ref, slab_ref, block, planes, channels, columns):
    base = pl.multiple_of((block * CY + 1) * channels, channels)
    for tap_row, cell_row, zs, ys in crop_tiles(planes, block, channels):
        patch_ref[pl.ds(tap_row, channels), pl.ds(cell_row * columns, columns)] = slab_ref[
            zs, pl.ds(base + ys * channels, channels), :
        ]


def conv_rows(weights, patch_ref, first, rows, out_channels, columns):
    taps = jnp.dot(
        weights,
        patch_ref[:, first * columns : (first + rows) * columns],
        preferred_element_type=F32,
    )
    results = []
    for row in range(rows):
        part = taps[:, row * columns : (row + 1) * columns]
        results.append(
            part[out_channels : 2 * out_channels]
            + shift_lanes(part[:out_channels], -1)
            + shift_lanes(part[2 * out_channels :], 1)
        )
    return results


def forward_kernel(dims, route_ref, param_ref, slab_ref, u_ref, stat_ref, patch, table, turned):
    planes, blocks, channels, out_channels, columns, slots = dims
    cell_rows = planes * CY
    cells = cell_rows * columns
    patch[...] = jnp.zeros_like(patch)
    table[...] = jnp.zeros_like(table)

    def step(block, carry):
        fill_patches(patch, slab_ref, block, planes, channels, columns)
        weights = param_ref[0 : 3 * out_channels, :]
        total = jnp.zeros((out_channels, columns), F32)
        for first in range(0, cell_rows, 2):
            rows = conv_rows(weights, patch, first, 2, out_channels, columns)
            for k, row in enumerate(rows):
                rounded = row.astype(BF16)
                u_ref[block, :, (first + k) * columns : (first + k + 1) * columns] = rounded
                total = total + rounded.astype(F32)
        total = jnp.sum(total, axis=1, keepdims=True)
        mean = total * (1.0 / cells)
        square = jnp.zeros((out_channels, columns), F32)
        for row in range(cell_rows):
            diff = u_ref[block, :, row * columns : (row + 1) * columns].astype(F32) - mean
            square = square + diff * diff
        square = jnp.sum(square, axis=1, keepdims=True)
        put_column(table, slice(0, out_channels), block, total)
        put_column(table, slice(out_channels, 2 * out_channels), block, square)
        return carry

    lax.fori_loop(0, blocks, step, 0)
    turned[...] = jnp.transpose(table[...])

    def route(slot, carry):
        block = route_ref[slot]
        entry = turned[pl.ds(jnp.maximum(block, 0), 1), :]
        stat_ref[pl.ds(slot, 1), :] = jnp.where(block >= 0, entry, 0.0)
        return carry

    lax.fori_loop(0, slots, route, 0)


def score_kernel(dims, param_ref, slab_ref, low_ref, high_ref, out_ref, patch):
    planes, blocks, channels, out_channels, columns, slots = dims
    height = blocks * CY
    group = 8
    taps = 3 * channels
    vectors = param_ref[3 * out_channels :, :LANES].astype(F32)
    gain, shift, head, mean, spread = (vectors[:, k : k + 1] for k in range(5))
    inverse = lax.rsqrt(spread + EPS)

    for z in range(planes):

        def step(number, carry, z=z):
            for row in range(group):
                start = pl.multiple_of((number * group + row) * channels, channels)
                for dz in range(3):
                    zs = z + dz - 1
                    where = pl.ds(start, taps)
                    if zs < 0:
                        piece = low_ref[where, :]
                    elif zs >= planes:
                        piece = high_ref[where, :]
                    else:
                        piece = slab_ref[zs, where, :]
                    patch[dz * taps : (dz + 1) * taps, row * columns : (row + 1) * columns] = piece
            weights = param_ref[0 : 3 * out_channels, :]
            lines = []
            for first in range(0, group, 2):
                for value in conv_rows(weights, patch, first, 2, out_channels, columns):
                    hidden = jnp.maximum(gain * ((value - mean) * inverse) + shift, 0.0)
                    lines.append(jnp.sum(head * hidden, axis=0, keepdims=True))
            out_ref[z, pl.ds(pl.multiple_of(number * group, group), group), :] = jnp.concatenate(
                lines, axis=0
            )
            return carry

        lax.fori_loop(0, height // group, step, 0)


def crop_row(u_ref, label_ref, block, row, columns, mu, inverse, vectors, count):
    gain, shift, head = vectors
    value = u_ref[block, :, row * columns : (row + 1) * columns].astype(F32)
    normal = (value - mu) * inverse
    before = gain * normal + shift
    hidden = jnp.maximum(before, 0.0)
    score = jnp.sum(head * hidden, axis=0, keepdims=True)
    residual = (score - label_ref[block, row : row + 1, :]) / count
    dbefore = jnp.where(before > 0, head * residual, 0.0)
    return normal, hidden, residual, dbefore


def sums_kernel(
    dims,
    route_ref,
    count_ref,
    param_ref,
    u_ref,
    label_ref,
    stat_ref,
    live_ref,
    counts_ref,
    sum_ref,
    norm_ref,
    vec_ref,
    square,
    table,
):
    planes, blocks, channels, out_channels, columns, slots = dims
    cell_rows = planes * CY
    cells = cell_rows * columns
    sources = stat_ref.shape[0]
    total = stat_ref[0]
    for s in range(1, sources):
        total = total + stat_ref[s]
    counts = counts_ref[...]
    mu = total / counts
    spread = jnp.zeros_like(mu)
    for s in range(sources):
        entry = stat_ref[s]
        diff = entry * (1.0 / cells) - mu
        spread = spread + (
            pltpu.roll(entry, LANES - out_channels, 1) + live_ref[s] * cells * (diff * diff)
        )
    inverse = lax.rsqrt(spread / counts + EPS)
    lane = lax.broadcasted_iota(jnp.int32, mu.shape, 1)
    square[...] = jnp.zeros_like(square)
    square[0:slots, :] = jnp.where(lane < out_channels, mu, pltpu.roll(inverse, out_channels, 1))
    norm_ref[...] = jnp.transpose(square[...])
    table[...] = jnp.zeros_like(table)
    vec_ref[...] = jnp.zeros_like(vec_ref)

    def step(slot, carry):
        block = route_ref[slot]

        @pl.when(block >= 0)
        def _():
            vec = param_ref[3 * out_channels :, :LANES].astype(F32)
            vectors = tuple(vec[:, k : k + 1] for k in range(3))
            pair = column(norm_ref[...], slot)
            mean, inv = pair[:out_channels], pair[out_channels:]
            count = count_ref[slot]
            first = jnp.zeros((out_channels, columns), F32)
            second, third = first, first
            for row in range(cell_rows):
                normal, hidden, residual, dbefore = crop_row(
                    u_ref, label_ref, block, row, columns, mean, inv, vectors, count
                )
                first = first + dbefore
                second = second + dbefore * normal
                third = third + hidden * residual
            put_column(
                table, slice(0, out_channels), slot, jnp.sum(first, axis=1, keepdims=True)
            )
            put_column(
                table,
                slice(out_channels, 2 * out_channels),
                slot,
                jnp.sum(second, axis=1, keepdims=True),
            )
            vec_ref[...] += third

        return carry

    lax.fori_loop(0, slots, step, 0)
    both = table[...]
    sums = jnp.sum(both, axis=1, keepdims=True)
    last = jnp.sum(vec_ref[...], axis=1, keepdims=True)
    wide = lax.broadcasted_iota(jnp.int32, vec_ref.shape, 1)
    vec_ref[...] = jnp.where(
        wide == 0,
        sums[out_channels:],
        jnp.where(wide == 1, sums[:out_channels], jnp.where(wide == 2, last, 0.0)),
    )
    square[...] = jnp.transpose(both)
    sum_ref[...] = square[0:slots, :]


def grad_kernel(
    dims,
    route_ref,
    count_ref,
    param_ref,
    slab_ref,
    u_ref,
    label_ref,
    sum_ref,
    counts_ref,
    norm_ref,
    grad_ref,
    patch,
    field,
    square,
    means,
):
    planes, blocks, channels, out_channels, columns, slots = dims
    cell_rows = planes * CY
    total = sum_ref[0]
    for s in range(1, sum_ref.shape[0]):
        total = total + sum_ref[s]
    square[...] = jnp.zeros_like(square)
    square[0:slots, :] = total / counts_ref[...]
    means[...] = jnp.transpose(square[...])
    patch[...] = jnp.zeros_like(patch)
    grad_ref[...] = jnp.zeros_like(grad_ref)

    def step(slot, carry):
        block = route_ref[slot]

        @pl.when(block >= 0)
        def _():
            vec = param_ref[3 * out_channels :, :LANES].astype(F32)
            vectors = tuple(vec[:, k : k + 1] for k in range(3))
            gain = vectors[0]
            pair = column(norm_ref[...], slot)
            mean, inv = pair[:out_channels], pair[out_channels:]
            pair = column(means[...], slot)
            first, second = gain * pair[:out_channels], gain * pair[out_channels:]
            count = count_ref[slot]
            fill_patches(patch, slab_ref, block, planes, channels, columns)
            for row in range(cell_rows):
                normal, hidden, residual, dbefore = crop_row(
                    u_ref, label_ref, block, row, columns, mean, inv, vectors, count
                )
                du = inv * (dbefore * gain - first - normal * second)
                du = du.astype(BF16).astype(F32)
                where = slice(row * columns, (row + 1) * columns)
                field[0:out_channels, where] = shift_lanes(du, 1).astype(BF16)
                field[out_channels : 2 * out_channels, where] = du.astype(BF16)
                field[2 * out_channels :, where] = shift_lanes(du, -1).astype(BF16)
            grad_ref[...] += lax.dot_general(
                field[...], patch[...], (((1,), (1,)), ((), ())), preferred_element_type=F32
            )

        return carry

    lax.fori_loop(0, slots, step, 0)


def spread_to_all(value, axis):
    count = lax.axis_size(axis)
    copies = jnp.broadcast_to(value[None], (count,) + value.shape)
    return lax.all_to_all(copies, axis, split_axis=0, concat_axis=0, tiled=True)


VM = pl.BlockSpec(memory_space=pltpu.VMEM)
SM = pl.BlockSpec(memory_space=pltpu.SMEM)


def call(kernel, dims, outs, ins, scratch, flops, args):
    return pl.pallas_call(
        functools.partial(kernel, dims),
        out_shape=outs,
        in_specs=ins,
        out_specs=jax.tree.map(lambda _: VM, outs),
        scratch_shapes=scratch,
        cost_estimate=pl.CostEstimate(flops=flops, bytes_accessed=1 << 22, transcendentals=0),
        compiler_params=pltpu.CompilerParams(vmem_limit_bytes=48 * 1024 * 1024),
    )(*args)


def per_device(features, labels, crop_block, weight, gain, shift, head, run_mean, run_var):
    slab = features[0]
    channels, planes, height, columns = slab.shape
    own_rows = weight.shape[0]
    devices = lax.axis_size("dev")
    own_index = lax.axis_index("dev")
    out_channels = own_rows * devices
    taps = 9 * channels
    blocks = height // CY
    cell_rows = planes * CY
    cells = cell_rows * columns
    table = crop_block[0]
    slots = table.shape[1]
    dims = (planes, blocks, channels, out_channels, columns, slots)

    weight_b = weight.astype(BF16).reshape(own_rows, 9, 3, channels).transpose(2, 0, 1, 3)
    vectors = jnp.stack([gain, shift, head, run_mean, run_var], 1).astype(BF16)
    vectors = jnp.pad(vectors, ((0, 0), (0, taps - vectors.shape[1])))
    own_params = jnp.concatenate([weight_b.reshape(3, own_rows, taps), vectors[None]], 0)
    params = spread_to_all(own_params, "dev").transpose(1, 0, 2, 3).reshape(4 * out_channels, taps)

    turned = jnp.pad(slab.transpose(1, 2, 0, 3), ((0, 0), (1, 1), (0, 0), (0, 0)))
    turned = turned.reshape(planes, (height + 2) * channels, columns)
    low = lax.ppermute(turned[planes - 1], "dev", [(i, i + 1) for i in range(devices - 1)])
    high = lax.ppermute(turned[0], "dev", [(i + 1, i) for i in range(devices - 1)])

    route = lax.dynamic_slice_in_dim(table, own_index, 1, 0)[0]
    live = (table >= 0).astype(F32)
    count = jnp.sum(live, 0) * cells
    counts = jnp.broadcast_to(count[:, None], (slots, LANES))
    live_wide = jnp.broadcast_to(live[:, :, None], live.shape + (LANES,))
    targets = labels[0].reshape(planes, blocks, CY, columns).transpose(1, 0, 2, 3)
    targets = targets.reshape(blocks, cell_rows, columns).astype(F32)

    shape = jax.ShapeDtypeStruct
    conv_flops = 2 * 27 * channels * out_channels * planes * height * columns
    patch = pltpu.VMEM((taps, cells), BF16)
    tile = pltpu.VMEM((LANES, LANES), F32)
    u, stats = call(
        forward_kernel,
        dims,
        (shape((blocks, out_channels, cells), BF16), shape((slots, LANES), F32)),
        [SM, VM, VM],
        [patch, tile, tile],
        conv_flops,
        (route, params, turned),
    )
    all_stats = spread_to_all(stats[None], "dev")
    all_stats = all_stats.reshape(devices, slots, LANES)
    scores = call(
        score_kernel,
        dims,
        shape((planes, height, columns), F32),
        [VM, VM, VM, VM],
        [pltpu.VMEM((taps, 8 * columns), BF16)],
        conv_flops,
        (params, turned, low, high),
    )
    sums, norms, vector_terms = call(
        sums_kernel,
        dims,
        (
            shape((slots, LANES), F32),
            shape((LANES, LANES), F32),
            shape((out_channels, columns), F32),
        ),
        [SM, SM, VM, VM, VM, VM, VM, VM],
        [tile, tile],
        conv_flops // 16,
        (route, count, params, u, targets, all_stats, live_wide, counts),
    )
    all_sums = spread_to_all(sums[None], "dev").reshape(devices, slots, LANES)
    terms = call(
        grad_kernel,
        dims,
        shape((3 * out_channels, taps), F32),
        [SM, SM, VM, VM, VM, VM, VM, VM, VM],
        [patch, pltpu.VMEM((3 * out_channels, cells), BF16), tile, tile],
        conv_flops,
        (route, count, params, turned, u, targets, all_sums, counts, norms),
    )
    terms = terms.reshape(3, devices, own_rows, taps).transpose(1, 0, 2, 3)
    vector_terms = jnp.pad(vector_terms, ((0, 0), (0, taps - columns)))
    vector_terms = vector_terms.reshape(devices, 1, own_rows, taps)
    packed = jnp.concatenate([terms, vector_terms], 1)
    packed = lax.all_to_all(packed, "dev", split_axis=0, concat_axis=0, tiled=True)
    part = jnp.sum(packed, 0)
    roles = lax.axis_size("role")
    total = part
    moving = part
    for _ in range(roles - 1):
        moving = lax.ppermute(moving, "role", [(i, (i + 1) % roles) for i in range(roles)])
        total = total + moving
    weight_grad = total[:3].reshape(3, own_rows, 9, channels).transpose(1, 2, 0, 3)
    return scores[None], weight_grad.reshape(own_rows, 27 * channels), total[3, :, :3]


def solution(mesh):
    in_specs = (
        P("role", None, "dev", None, None),
        P("role", "dev", None, None),
        P("role", None, None),
        P("dev", None),
        P("dev"),
        P("dev"),
        P("dev"),
        P("dev"),
        P("dev"),
    )
    out_specs = (P("role", "dev", None, None), P("dev", None), P("dev", None))
    return jax.shard_map(
        per_device, mesh=mesh, in_specs=in_specs, out_specs=out_specs, check_vma=False
    )
```

time: 454 us -> 113 us (0.25)
  the two profiles are of different devices: /device:TPU:0 before, /device:TPU:21 now
where the time goes in v1:
time: 113 us; the launch traced here: 112 us
  starting transfers between devices  35.7 us (32%)
  Pallas kernels  26.2 us (23%)
  waiting for transfers between devices  25.5 us (23%)
  local copies, waits for them, and re-layouts  18 us (16%)
  other arithmetic  5.57 us (5%)
    pallas_call x4, Pallas kernels, call(): pl.pallas_call(functools.partial(kernel, dims), out_shape=outs, in_specs=...  26.2 us
    all_to_all x3, starting transfers between devices, spread_to_all(): return lax.all_to_all(copies, axis, split_axis=0, concat_axis=0, tiled=True)  20.3 us
    all_to_all x3, waiting for transfers between devices, spread_to_all(): return lax.all_to_all(copies, axis, split_axis=0, concat_axis=0, tiled=True)  10.4 us
    all_to_all x1, starting transfers between devices, per_device(): lax.all_to_all(packed, 'dev', split_axis=0, concat_axis=0, tiled=True)  10.1 us
    ppermute x1, waiting for transfers between devices, per_device(): lax.ppermute(turned[planes - 1], 'dev', [(i, i + 1) for i in range(device...  7.23 us
    unnamed x19, local copies, waits for them, and re-layouts  6.29 us
    ppermute x1, waiting for transfers between devices, per_device(): lax.ppermute(turned[0], 'dev', [(i + 1, i) for i in range(devices - 1)])  4.17 us
    all_to_all x1, waiting for transfers between devices, per_device(): lax.all_to_all(packed, 'dev', split_axis=0, concat_axis=0, tiled=True)  3.72 us
  transfers between devices with their start and end apart: 7, of which 6 were waited for; matrix products, arithmetic and copies ran while one was open for 7% of the time, Pallas kernels for 8%

profile of v1, /device:TPU:21, one launch (start us, length us, event | category | flops | bytes accessed | tf_op | source)
XLA Modules:
  0.0 111.8 jit_solution(2446581421157665628)
XLA Ops:
  0.6 0.7 convert_element_type.29
  1.6 0.7 convert_bitcast_fusion.5
  2.3 0.7 convert_bitcast_fusion.4
  3.0 0.1 copy.31
  3.1 0.7 convert_bitcast_fusion.3
  3.8 0.1 copy.32
  3.9 0.7 convert_bitcast_fusion.2
  4.5 0.1 copy.33
  4.6 0.7 convert_bitcast_fusion.1
  5.5 0.7 broadcast_in_dim.15
  6.3 6.5 %all-to-all-start = ((bf16[16,4,4,288]{3,2,1,0:T(4,128)(2,1)}), bf16[16,4,4,288]{3,2,1,0:T(4,128)(2,1)S(1)}, u32[]{:S(2)}, u32[]{:S(2)}) async-start(bf16[16,4,4,288]{3,2,1,0:T(4,128)(2,1)} %broadcast_in_dim.15), calls=%async_computation | async-start | bytes 393216 | tf_op jit(solution)/shard_map/all_to_all | solution.py:312
  12.8 0.7 dynamic-slice_bitcast_fusion.route_ref
  13.4 1.9 %copy.44 = bf16[2,64,32,128]{3,2,1,0:T(8,128)(2,1)S(1)} copy(bf16[2,64,32,128]{3,1,0,2:T(8,128)(2,1)} %bitcast.48) | data formatting | bytes 2097152
  15.4 0.2 pad.13.clone
  15.6 0.5 copy-done.8
  16.1 0.6 convert_bitcast_fusion
  16.7 2.4 %all-to-all-done = bf16[16,4,4,288]{3,2,1,0:T(4,128)(2,1)S(1)} async-done(((bf16[16,4,4,288]{3,2,1,0:T(4,128)(2,1)}), bf16[16,4,4,288]{3,2,1,0:T(4,128)(2,1)S(1)}, u32[]{:S(2)}, u32[]{:S(2)}) %all-to-all-start) | async-done | bytes 147488 | tf_op jit(solution)/shard_map/all_to_all | solution.py:312
  19.2 11.1 %shard_map.113 = (bf16[16,64,1024]{2,1,0:T(8,128)(2,1)S(1)}, f32[16,128]{1,0:T(8,128)S(1)}) custom-call(s32[16]{0:T(128)S(1)} %dynamic-slice_bitcast_fusion.route_ref, bf16[256,288]{1,0:T(8,128)(2,1)S(1)} %reshape.68.param_ref, bf16[2,2112,128]{2,1,0:T(8,128)(2,1)S(1)} %bitcast.41), custom_call_target="tpu_custom_call" | custom-call | flops 1811939328 | bytes 4194304 | tf_op jit(solution)/shard_map/pallas_call | solution.py:320
  30.4 0.7 broadcast_in_dim.17
  31.1 6.1 %all-to-all-start.1 = ((f32[16,1,16,128]{3,2,1,0:T(8,128)}), f32[16,1,16,128]{3,2,1,0:T(8,128)S(1)}, u32[]{:S(2)}, u32[]{:S(2)}) async-start(f32[16,1,16,128]{3,2,1,0:T(8,128)} %broadcast_in_dim.17), calls=%async_computation.1 | async-start | bytes 262144 | tf_op jit(solution)/shard_map/all_to_all | solution.py:312
  37.2 0.6 copy.39
  37.9 4.8 %all-to-all-done.1 = f32[16,1,16,128]{3,2,1,0:T(8,128)S(1)} async-done(((f32[16,1,16,128]{3,2,1,0:T(8,128)}), f32[16,1,16,128]{3,2,1,0:T(8,128)S(1)}, u32[]{:S(2)}, u32[]{:S(2)}) %all-to-all-start.1) | async-done | bytes 131104 | tf_op jit(solution)/shard_map/all_to_all | solution.py:312
  42.7 0.8 broadcast_in_dim.18.live_ref
  43.5 0.8 copy-done.1
  44.3 2.5 %shard_map.114 = (f32[16,128]{1,0:T(8,128)S(1)}, f32[128,128]{1,0:T(8,128)S(1)}, f32[64,128]{1,0:T(8,128)S(1)}) custom-call(s32[16]{0:T(128)S(1)} %dynamic-slice_bitcast_fusion.route_ref, f32[16]{0:T(128)S(1)} %broadcast_multiply_fusion.count_ref, bf16[256,288]{1,0:T(8,128)(2,1)S(1)} %reshape.68.param_ref, bf16[16,64,1024]{2,1,0:T(8,128)(2,1)S(1)} %get-tuple-element.8.u_ref, ...), custom_call_target="tpu_custom_call" | custom-call | flops 113246208 | bytes 4194304 | tf_op jit(solution)/shard_map/pallas_call | solution.py:320
  46.8 0.6 copy-done.3
  47.5 0.7 broadcast_in_dim.40
  48.1 7.7 %all-to-all-start.2 = ((f32[16,1,16,128]{3,2,1,0:T(8,128)}), f32[16,1,16,128]{3,2,1,0:T(8,128)S(1)}, u32[]{:S(2)}, u32[]{:S(2)}) async-start(f32[16,1,16,128]{3,2,1,0:T(8,128)} %broadcast_in_dim.40), calls=%async_computation.2 | async-start | bytes 262144 | tf_op jit(solution)/shard_map/all_to_all | solution.py:312
  55.8 0.6 pad.14
  56.5 1.6 %reshape.73 = f32[16,1,4,288]{3,2,0,1:T(4,128)} reshape(f32[64,288]{1,0:T(8,128)} %pad.14) | data formatting | bytes 147456 | tf_op jit(solution)/shard_map/reshape | solution.py:414
  58.0 3.2 %all-to-all-done.2 = f32[16,1,16,128]{3,2,1,0:T(8,128)S(1)} async-done(((f32[16,1,16,128]{3,2,1,0:T(8,128)}), f32[16,1,16,128]{3,2,1,0:T(8,128)S(1)}, u32[]{:S(2)}, u32[]{:S(2)}) %all-to-all-start.2) | async-done | bytes 131104 | tf_op jit(solution)/shard_map/all_to_all | solution.py:312
  61.3 0.8 copy-done.2
  62.1 0.8 copy-done.4
  62.9 3.6 %shard_map.115 = f32[192,288]{1,0:T(8,128)S(1)} custom-call(s32[16]{0:T(128)S(1)} %dynamic-slice_bitcast_fusion.route_ref, f32[16]{0:T(128)S(1)} %broadcast_multiply_fusion.count_ref, bf16[256,288]{1,0:T(8,128)(2,1)S(1)} %reshape.68.param_ref, bf16[2,2112,128]{2,1,0:T(8,128)(2,1)S(1)} %bitcast.42, bf16[16,64,1024]{2,1,0:T(8,128)(2,1)S(1)} %get-tuple-element.8.u_ref, ...), custom_call_target="tpu_custom_call" | custom-call | flops 1811939328 | bytes 4194304 | tf_op jit(solution)/shard_map/pallas_call | solution.py:320
  66.5 0.7 copy-done
  67.2 1.1 reshape.72
  68.4 0.8 pad_maximum_fusion
  69.2 10.1 %all-to-all-start.3 = ((f32[16,4,4,288]{3,2,1,0:T(4,128)}), f32[16,4,4,288]{3,2,1,0:T(4,128)S(1)}, u32[]{:S(2)}, u32[]{:S(2)}) async-start(f32[16,4,4,288]{3,2,1,0:T(4,128)} %pad_maximum_fusion), calls=%async_computation.3 | async-start | bytes 786432 | tf_op jit(solution)/shard_map/all_to_all | solution.py:416
  79.3 0.5 pad_slice_fusion
  79.9 3.3 %collective-permute-start = (bf16[2112,128]{1,0:T(8,128)(2,1)S(1)}, bf16[2112,128]{1,0:T(8,128)(2,1)S(1)}, u32[]{:S(2)}, u32[]{:S(2)}) collective-permute-start(bf16[2112,128]{1,0:T(8,128)(2,1)S(1)} %bitcast.52), channel_id=1, source_target_pairs={{0,1},{1,2},{2,3},{3,4},{4,5},{5,6},{6,7},{7,8},{8,9},{9,10},{10,1... | collective-permute-start | bytes 1622024 | tf_op jit(solution)/shard_map/ppermute | solution.py:354
  83.3 0.9 copy.38
  84.2 1.9 %collective-permute-start.1 = (bf16[2112,128]{1,0:T(8,128)(2,1)}, bf16[2112,128]{1,0:T(8,128)(2,1)S(1)}, u32[]{:S(2)}, u32[]{:S(2)}) collective-permute-start(bf16[2112,128]{1,0:T(8,128)(2,1)} %bitcast.12), channel_id=1, source_target_pairs={{1,0},{2,1},{3,2},{4,3},{5,4},{6,5},{7,6},{8,7},{9,8},{10,9},{11,1... | collective-permute-start | bytes 1622024 | tf_op jit(solution)/shard_map/ppermute | solution.py:355
  86.1 3.7 %all-to-all-done.3 = f32[16,4,4,288]{3,2,1,0:T(4,128)S(1)} async-done(((f32[16,4,4,288]{3,2,1,0:T(4,128)}), f32[16,4,4,288]{3,2,1,0:T(4,128)S(1)}, u32[]{:S(2)}, u32[]{:S(2)}) %all-to-all-start.3) | async-done | bytes 294944 | tf_op jit(solution)/shard_map/all_to_all | solution.py:416
  90.0 7.2 %collective-permute-done.low_ref = bf16[2112,128]{1,0:T(8,128)(2,1)S(1)} collective-permute-done((bf16[2112,128]{1,0:T(8,128)(2,1)S(1)}, bf16[2112,128]{1,0:T(8,128)(2,1)S(1)}, u32[]{:S(2)}, u32[]{:S(2)}) %collective-permute-start) | collective-permute-done | bytes 540704 | tf_op jit(solution)/shard_map/ppermute | solution.py:354
  97.2 4.2 %collective-permute-done.1.high_ref = bf16[2112,128]{1,0:T(8,128)(2,1)S(1)} collective-permute-done((bf16[2112,128]{1,0:T(8,128)(2,1)}, bf16[2112,128]{1,0:T(8,128)(2,1)S(1)}, u32[]{:S(2)}, u32[]{:S(2)}) %collective-permute-start.1) | collective-permute-done | bytes 540704 | tf_op jit(solution)/shard_map/ppermute | solution.py:355
  101.4 9.0 %shard_map.112 = f32[2,64,128]{2,1,0:T(8,128)} custom-call(bf16[256,288]{1,0:T(8,128)(2,1)S(1)} %reshape.68.param_ref, bf16[2,2112,128]{2,1,0:T(8,128)(2,1)S(1)} %bitcast.43, bf16[2112,128]{1,0:T(8,128)(2,1)S(1)} %collective-permute-done.low_ref, bf16[2112,128]{1,0:T(8,128)(2,1)S(1)} %collective-permute-done.1.high_ref), custom_call_target="tpu_custom_call" | custom-call | flops 1811939328 | bytes 4194304 | tf_op jit(solution)/shard_map/pallas_call | solution.py:320
  110.4 0.6 slice_bitcast_fusion
  111.1 0.7 reshape.75
  (34 shorter events, 1.2 us)
Async XLA Ops:
  6.3 12.8 %all-to-all-start = ((bf16[16,4,4,288]{3,2,1,0:T(4,128)(2,1)}), bf16[16,4,4,288]{3,2,1,0:T(4,128)(2,1)S(1)}, u32[]{:S(2)}, u32[]{:S(2)}) async-start(bf16[16,4,4,288]{3,2,1,0:T(4,128)(2,1)} %broadcast_in_dim.15), calls=%async_computation | async-start | bytes 393216 | tf_op jit(solution)/shard_map/all_to_all | solution.py:312
  15.3 0.7 copy-start.8
  19.2 18.0 %copy-start.7 = (bf16[1,2,64,128]{3,2,1,0:T(8,128)(2,1)S(1)}, bf16[1,2,64,128]{3,2,1,0:T(8,128)(2,1)}, u32[]{:S(2)}) copy-start(bf16[1,2,64,128]{3,2,1,0:T(8,128)(2,1)} %param.10) | copy-start | bytes 98308
  31.1 11.6 %all-to-all-start.1 = ((f32[16,1,16,128]{3,2,1,0:T(8,128)}), f32[16,1,16,128]{3,2,1,0:T(8,128)S(1)}, u32[]{:S(2)}, u32[]{:S(2)}) async-start(f32[16,1,16,128]{3,2,1,0:T(8,128)} %broadcast_in_dim.17), calls=%async_computation.1 | async-start | bytes 262144 | tf_op jit(solution)/shard_map/all_to_all | solution.py:312
  43.5 0.8 copy-start.1
  46.8 0.7 copy-start.3
  48.1 13.1 %all-to-all-start.2 = ((f32[16,1,16,128]{3,2,1,0:T(8,128)}), f32[16,1,16,128]{3,2,1,0:T(8,128)S(1)}, u32[]{:S(2)}, u32[]{:S(2)}) async-start(f32[16,1,16,128]{3,2,1,0:T(8,128)} %broadcast_in_dim.40), calls=%async_computation.2 | async-start | bytes 262144 | tf_op jit(solution)/shard_map/all_to_all | solution.py:312
  61.2 0.8 copy-start.2
  62.1 0.8 copy-start.4
  66.5 0.7 copy-start
  67.2 1.1 %copy-start.6 = (f32[16,1,4,288]{3,2,0,1:T(4,128)S(1)}, f32[16,1,4,288]{3,2,0,1:T(4,128)}, u32[]{:S(2)}) copy-start(f32[16,1,4,288]{3,2,0,1:T(4,128)} %reshape.73) | copy-start | bytes 221188
  68.3 11.0 %copy-start.5 = (bf16[1,32,2,64,128]{4,3,2,1,0:T(8,128)(2,1)S(1)}, bf16[1,32,2,64,128]{4,3,2,1,0:T(8,128)(2,1)}, u32[]{:S(2)}) copy-start(bf16[1,32,2,64,128]{4,3,2,1,0:T(8,128)(2,1)} %param.9) | copy-start | bytes 3145732
  69.2 20.6 %all-to-all-start.3 = ((f32[16,4,4,288]{3,2,1,0:T(4,128)}), f32[16,4,4,288]{3,2,1,0:T(4,128)S(1)}, u32[]{:S(2)}, u32[]{:S(2)}) async-start(f32[16,4,4,288]{3,2,1,0:T(4,128)} %pad_maximum_fusion), calls=%async_computation.3 | async-start | bytes 786432 | tf_op jit(solution)/shard_map/all_to_all | solution.py:416
  79.9 17.3 %collective-permute-start = (bf16[2112,128]{1,0:T(8,128)(2,1)S(1)}, bf16[2112,128]{1,0:T(8,128)(2,1)S(1)}, u32[]{:S(2)}, u32[]{:S(2)}) collective-permute-start(bf16[2112,128]{1,0:T(8,128)(2,1)S(1)} %bitcast.52), channel_id=1, source_target_pairs={{0,1},{1,2},{2,3},{3,4},{4,5},{5,6},{6,7},{7,8},{8,9},{9,10},{10,1... | collective-permute-start | bytes 1622024 | tf_op jit(solution)/shard_map/ppermute | solution.py:354
  84.2 17.2 %collective-permute-start.1 = (bf16[2112,128]{1,0:T(8,128)(2,1)}, bf16[2112,128]{1,0:T(8,128)(2,1)S(1)}, u32[]{:S(2)}, u32[]{:S(2)}) collective-permute-start(bf16[2112,128]{1,0:T(8,128)(2,1)} %bitcast.12), channel_id=1, source_target_pairs={{1,0},{2,1},{3,2},{4,3},{5,4},{6,5},{7,6},{8,7},{9,8},{10,9},{11,1... | collective-permute-start | bytes 1622024 | tf_op jit(solution)/shard_map/ppermute | solution.py:355
  89.9 20.5 %collective-permute-start.2 = (f32[4,4,288]{2,1,0:T(4,128)S(1)}, f32[4,4,288]{2,1,0:T(4,128)S(1)}, u32[]{:S(2)}, u32[]{:S(2)}) collective-permute-start(f32[4,4,288]{2,1,0:T(4,128)S(1)} %reduce_sum.19), channel_id=1, source_target_pairs={{0,16},{16,0},{1,17},{17,1},{2,18},{18,2},{3,19},{19,3},{4,20},{20... | collective-permute-start | bytes 55304 | tf_op jit(solution)/shard_map/ppermute | solution.py:422

commit v2 on v1

v2 whole, which is shorter than its diff:
```python
import functools

import jax
import jax.numpy as jnp
from jax import lax
from jax.experimental import pallas as pl
from jax.experimental.pallas import tpu as pltpu
from jax.sharding import PartitionSpec as P

CY = 4
EPS = 1e-05
LANES = 128
F32 = jnp.float32
BF16 = jnp.bfloat16


def shift_lanes(value, offset):
    lane = lax.broadcasted_iota(jnp.int32, value.shape, 1)
    width = value.shape[1]
    if offset < 0:
        return jnp.where(lane == 0, 0.0, pltpu.roll(value, 1, 1))
    return jnp.where(lane == width - 1, 0.0, pltpu.roll(value, width - 1, 1))


def column(table, index):
    lane = lax.broadcasted_iota(jnp.int32, table.shape, 1)
    return jnp.sum(jnp.where(lane == index, table, 0.0), axis=1, keepdims=True)


def put_column(ref, rows, index, value):
    part = ref[rows, :]
    lane = lax.broadcasted_iota(jnp.int32, part.shape, 1)
    ref[rows, :] = jnp.where(lane == index, value, part)


def crop_tiles(planes, block, channels):
    for z in range(planes):
        for y in range(CY):
            cell_row = z * CY + y
            for dz in range(3):
                for dy in range(3):
                    zs, ys = z + dz - 1, y + dy - 1
                    if 0 <= zs < planes and 0 <= ys < CY:
                        yield (dz * 3 + dy) * channels, cell_row, zs, ys


def fill_patches(patch_ref, slab_ref, block, planes, channels, columns):
    base = pl.multiple_of((block * CY + 1) * channels, channels)
    for tap_row, cell_row, zs, ys in crop_tiles(planes, block, channels):
        patch_ref[pl.ds(tap_row, channels), pl.ds(cell_row * columns, columns)] = slab_ref[
            zs, pl.ds(base + ys * channels, channels), :
        ]


def conv_rows(weights, patch_ref, first, rows, out_channels, columns):
    taps = jnp.dot(
        weights,
        patch_ref[:, first * columns : (first + rows) * columns],
        preferred_element_type=F32,
    )
    results = []
    for row in range(rows):
        part = taps[:, row * columns : (row + 1) * columns]
        results.append(
            part[out_channels : 2 * out_channels]
            + shift_lanes(part[:out_channels], -1)
            + shift_lanes(part[2 * out_channels :], 1)
        )
    return results


def peer_of(me, step, count):
    return lax.rem(me + step, count)


def greet(axes):
    barrier = pltpu.get_barrier_semaphore()
    total = 0
    for axis, count in axes:
        me = lax.axis_index(axis)

        def tell(step, carry, axis=axis, count=count, me=me):
            pl.semaphore_signal(
                barrier,
                inc=1,
                device_id={axis: peer_of(me, step, count)},
                device_id_type=pl.DeviceIdType.MESH,
            )
            return carry

        lax.fori_loop(1, count, tell, 0)
        total += count - 1
    pl.semaphore_wait(barrier, total)


def to_peer(axis, count, step, source, target, sends, receives):
    me = lax.axis_index(axis)
    peer = peer_of(me, step, count)
    return pltpu.make_async_remote_copy(
        src_ref=source(peer),
        dst_ref=target.at[me],
        send_sem=sends.at[step],
        recv_sem=receives.at[step],
        device_id={axis: peer},
        device_id_type=pl.DeviceIdType.MESH,
    )


def start_all(*parts):
    def one(step, carry):
        to_peer(parts[0], parts[1], step, *parts[2:]).start()
        return carry

    lax.fori_loop(1, parts[1], one, 0)


def wait_all(*parts):
    def one(step, carry):
        to_peer(parts[0], parts[1], step, *parts[2:]).wait()
        return carry

    lax.fori_loop(1, parts[1], one, 0)


def one_hot(rows, columns, target):
    row = lax.broadcasted_iota(jnp.int32, (rows, columns), 0)
    return (lax.broadcasted_iota(jnp.int32, (rows, columns), 1) == target(row)).astype(F32)


def score_plane(dims, z, param_ref, slab_ref, low_ref, high_ref, out_ref, patch):
    planes, blocks, channels, out_channels, columns, slots = dims
    height = blocks * CY
    group = 8
    taps = 3 * channels
    vectors = param_ref[3 * out_channels :, :LANES].astype(F32)
    gain, shift, head, mean, spread = (vectors[:, k : k + 1] for k in range(5))
    inverse = lax.rsqrt(spread + EPS)

    def step(number, carry):
        for row in range(group):
            start = pl.multiple_of((number * group + row) * channels, channels)
            for dz in range(3):
                zs = z + dz - 1
                where = pl.ds(start, taps)
                if zs < 0:
                    piece = low_ref[where, :]
                elif zs >= planes:
                    piece = high_ref[where, :]
                else:
                    piece = slab_ref[zs, where, :]
                patch[dz * taps : (dz + 1) * taps, row * columns : (row + 1) * columns] = piece
        weights = param_ref[0 : 3 * out_channels, :]
        lines = []
        for first in range(0, group, 2):
            for value in conv_rows(weights, patch, first, 2, out_channels, columns):
                hidden = jnp.maximum(gain * ((value - mean) * inverse) + shift, 0.0)
                lines.append(jnp.sum(head * hidden, axis=0, keepdims=True))
        out_ref[pl.ds(pl.multiple_of(number * group, group), group), :] = jnp.concatenate(
            lines, axis=0
        )
        return carry

    lax.fori_loop(0, height // group, step, 0)


def forward_kernel(
    dims,
    count,
    own_rows,
    route_ref,
    gain_ref,
    shift_ref,
    head_ref,
    mean_ref,
    spread_ref,
    weight_ref,
    slab_ref,
    live_ref,
    counts_ref,
    param_ref,
    u_ref,
    norm_ref,
    high_out,
    score_ref,
    patch,
    table,
    turned,
    own,
    held,
    stat,
    stats,
    low,
    high,
    sends,
    receives,
    stat_sends,
    stat_receives,
    halo_sends,
    halo_receives,
):
    planes, blocks, channels, out_channels, columns, slots = dims
    cell_rows = planes * CY
    cells = cell_rows * columns
    me = lax.axis_index("dev")
    rows = own.shape[0]
    tile = weight_ref[...]
    row = lax.broadcasted_iota(jnp.int32, tile.shape, 0)
    lane = lax.broadcasted_iota(jnp.int32, tile.shape, 1)
    for k, ref in enumerate((gain_ref, shift_ref, head_ref, mean_ref, spread_ref)):
        for o in range(own_rows):
            tile = jnp.where((row == 3 * own_rows + o) & (lane == k), ref[o], tile)
    own[...] = tile.astype(BF16)
    greet((("dev", count),))
    exchange = ("dev", count, lambda peer: own, held, sends, receives)
    start_all(*exchange)

    def halo(way):
        return pltpu.make_async_remote_copy(
            src_ref=slab_ref.at[planes - 1 if way == 0 else 0],
            dst_ref=low if way == 0 else high,
            send_sem=halo_sends.at[way],
            recv_sem=halo_receives.at[way],
            device_id={"dev": lax.rem(me + (1 if way == 0 else count - 1), count)},
            device_id_type=pl.DeviceIdType.MESH,
        )

    @pl.when(me < count - 1)
    def _():
        halo(0).start()

    @pl.when(me > 0)
    def _():
        halo(1).start()

    @pl.when(me == 0)
    def _():
        low[...] = jnp.zeros_like(low)

    @pl.when(me == count - 1)
    def _():
        high[...] = jnp.zeros_like(high)

    held[me] = own[...]
    patch[...] = jnp.zeros_like(patch)
    table[...] = jnp.zeros_like(table)
    order = one_hot(
        4 * out_channels,
        count * rows,
        lambda r: (r % out_channels) // own_rows * rows
        + r // out_channels * own_rows
        + r % own_rows,
    ).astype(BF16)
    wait_all(*exchange)
    param_ref[...] = jnp.dot(
        order, held[...].reshape(count * rows, -1), preferred_element_type=F32
    ).astype(BF16)

    def step(block, carry):
        fill_patches(patch, slab_ref, block, planes, channels, columns)
        weights = param_ref[0 : 3 * out_channels, :]
        total = jnp.zeros((out_channels, columns), F32)
        for first in range(0, cell_rows, 2):
            lines = conv_rows(weights, patch, first, 2, out_channels, columns)
            for k, line in enumerate(lines):
                rounded = line.astype(BF16)
                u_ref[block, :, (first + k) * columns : (first + k + 1) * columns] = rounded
                total = total + rounded.astype(F32)
        total = jnp.sum(total, axis=1, keepdims=True)
        mean = total * (1.0 / cells)
        square = jnp.zeros((out_channels, columns), F32)
        for r in range(cell_rows):
            diff = u_ref[block, :, r * columns : (r + 1) * columns].astype(F32) - mean
            square = square + diff * diff
        square = jnp.sum(square, axis=1, keepdims=True)
        put_column(table, slice(0, out_channels), block, total)
        put_column(table, slice(out_channels, 2 * out_channels), block, square)
        return carry

    lax.fori_loop(0, blocks, step, 0)
    turned[...] = jnp.transpose(table[...])

    def route(slot, carry):
        block = route_ref[slot]
        entry = turned[pl.ds(jnp.maximum(block, 0), 1), :]
        stat[pl.ds(slot, 1), :] = jnp.where(block >= 0, entry, 0.0)
        return carry

    lax.fori_loop(0, slots, route, 0)
    exchange = ("dev", count, lambda peer: stat, stats, stat_sends, stat_receives)
    start_all(*exchange)
    stats[me] = stat[...]

    @pl.when(me < count - 1)
    def _():
        halo(0).wait_send()
        halo(1).wait_recv()

    @pl.when(me > 0)
    def _():
        halo(1).wait_send()
        halo(0).wait_recv()

    high_out[...] = high[...]
    score_plane(dims, 0, param_ref, slab_ref, low, high, score_ref.at[0], patch)
    for z in range(1, planes - 1):
        score_plane(dims, z, param_ref, slab_ref, low, high, score_ref.at[z], patch)
    wait_all(*exchange)

    total = stats[0]
    for s in range(1, count):
        total = total + stats[s]
    counts = counts_ref[...]
    mu = total / counts
    spread = jnp.zeros_like(mu)
    for s in range(count):
        entry = stats[s]
        diff = entry * (1.0 / cells) - mu
        spread = spread + (
            pltpu.roll(entry, LANES - out_channels, 1) + live_ref[s] * cells * (diff * diff)
        )
    inverse = lax.rsqrt(spread / counts + EPS)
    wide = lax.broadcasted_iota(jnp.int32, mu.shape, 1)
    table[...] = jnp.zeros_like(table)
    table[0:slots, :] = jnp.where(wide < out_channels, mu, pltpu.roll(inverse, out_channels, 1))
    norm_ref[...] = jnp.transpose(table[...])


def means_kernel(
    dims,
    count,
    param_ref,
    slab_ref,
    high_ref,
    sum_ref,
    counts_ref,
    mean_ref,
    score_ref,
    patch,
    table,
    held,
    sends,
    receives,
):
    planes, slots = dims[0], dims[5]
    greet((("dev", count),))
    exchange = ("dev", count, lambda peer: sum_ref, held, sends, receives)
    start_all(*exchange)
    held[lax.axis_index("dev")] = sum_ref[...]
    score_plane(dims, planes - 1, param_ref, slab_ref, high_ref, high_ref, score_ref, patch)
    wait_all(*exchange)
    total = held[0]
    for s in range(1, count):
        total = total + held[s]
    table[...] = jnp.zeros_like(table)
    table[0:slots, :] = total / counts_ref[...]
    mean_ref[...] = jnp.transpose(table[...])


def scatter_kernel(
    count, roles, chunk_ref, out_ref, held, part, others, sends, receives, role_sends, role_receives
):
    me = lax.axis_index("dev")
    greet((("dev", count), ("role", roles)))
    exchange = ("dev", count, lambda peer: chunk_ref.at[peer], held, sends, receives)
    start_all(*exchange)
    held[me] = chunk_ref[me]
    wait_all(*exchange)
    total = held[0]
    for s in range(1, count):
        total = total + held[s]
    part[...] = total
    exchange = ("role", roles, lambda peer: part, others, role_sends, role_receives)
    start_all(*exchange)
    others[lax.axis_index("role")] = total
    wait_all(*exchange)
    total = others[0]
    for r in range(1, roles):
        total = total + others[r]
    out_ref[...] = total


def crop_row(u_ref, label_ref, block, row, columns, mu, inverse, vectors, count):
    gain, shift, head = vectors
    value = u_ref[block, :, row * columns : (row + 1) * columns].astype(F32)
    normal = (value - mu) * inverse
    before = gain * normal + shift
    hidden = jnp.maximum(before, 0.0)
    score = jnp.sum(head * hidden, axis=0, keepdims=True)
    residual = (score - label_ref[block, row : row + 1, :]) / count
    dbefore = jnp.where(before > 0, head * residual, 0.0)
    return normal, hidden, residual, dbefore


def sums_kernel(
    dims,
    route_ref,
    count_ref,
    param_ref,
    u_ref,
    label_ref,
    norm_ref,
    sum_ref,
    vec_ref,
    square,
    table,
):
    planes, blocks, channels, out_channels, columns, slots = dims
    cell_rows = planes * CY
    table[...] = jnp.zeros_like(table)
    vec_ref[...] = jnp.zeros_like(vec_ref)

    def step(slot, carry):
        block = route_ref[slot]

        @pl.when(block >= 0)
        def _():
            vec = param_ref[3 * out_channels :, :LANES].astype(F32)
            vectors = tuple(vec[:, k : k + 1] for k in range(3))
            pair = column(norm_ref[...], slot)
            mean, inv = pair[:out_channels], pair[out_channels:]
            cell_count = count_ref[slot]
            first = jnp.zeros((out_channels, columns), F32)
            second, third = first, first
            for row in range(cell_rows):
                normal, hidden, residual, dbefore = crop_row(
                    u_ref, label_ref, block, row, columns, mean, inv, vectors, cell_count
                )
                first = first + dbefore
                second = second + dbefore * normal
                third = third + hidden * residual
            put_column(
                table, slice(0, out_channels), slot, jnp.sum(first, axis=1, keepdims=True)
            )
            put_column(
                table,
                slice(out_channels, 2 * out_channels),
                slot,
                jnp.sum(second, axis=1, keepdims=True),
            )
            vec_ref[...] += third

        return carry

    lax.fori_loop(0, slots, step, 0)
    both = table[...]
    sums = jnp.sum(both, axis=1, keepdims=True)
    last = jnp.sum(vec_ref[...], axis=1, keepdims=True)
    wide = lax.broadcasted_iota(jnp.int32, vec_ref.shape, 1)
    vec_ref[...] = jnp.where(
        wide == 0,
        sums[out_channels:],
        jnp.where(wide == 1, sums[:out_channels], jnp.where(wide == 2, last, 0.0)),
    )
    square[...] = jnp.transpose(both)
    sum_ref[...] = square[0:slots, :]


def grad_kernel(
    dims,
    route_ref,
    count_ref,
    param_ref,
    slab_ref,
    u_ref,
    label_ref,
    norm_ref,
    means,
    vec_ref,
    pack_ref,
    patch,
    field,
    grad_ref,
):
    planes, blocks, channels, out_channels, columns, slots = dims
    cell_rows = planes * CY
    count, rows, taps = pack_ref.shape
    own_rows = out_channels // count
    patch[...] = jnp.zeros_like(patch)
    grad_ref[...] = jnp.zeros_like(grad_ref)

    def step(slot, carry):
        block = route_ref[slot]

        @pl.when(block >= 0)
        def _():
            vec = param_ref[3 * out_channels :, :LANES].astype(F32)
            vectors = tuple(vec[:, k : k + 1] for k in range(3))
            gain = vectors[0]
            pair = column(norm_ref[...], slot)
            mean, inv = pair[:out_channels], pair[out_channels:]
            pair = column(means[...], slot)
            first, second = gain * pair[:out_channels], gain * pair[out_channels:]
            cell_count = count_ref[slot]
            fill_patches(patch, slab_ref, block, planes, channels, columns)
            for row in range(cell_rows):
                normal, hidden, residual, dbefore = crop_row(
                    u_ref, label_ref, block, row, columns, mean, inv, vectors, cell_count
                )
                du = inv * (dbefore * gain - first - normal * second)
                du = du.astype(BF16).astype(F32)
                where = slice(row * columns, (row + 1) * columns)
                field[0:out_channels, where] = shift_lanes(du, 1).astype(BF16)
                field[out_channels : 2 * out_channels, where] = du.astype(BF16)
                field[2 * out_channels :, where] = shift_lanes(du, -1).astype(BF16)
            grad_ref[0 : 3 * out_channels, :] += lax.dot_general(
                field[...], patch[...], (((1,), (1,)), ((), ())), preferred_element_type=F32
            )

        return carry

    lax.fori_loop(0, slots, step, 0)
    grad_ref[3 * out_channels :, 0:LANES] = vec_ref[...]
    order = one_hot(
        count * rows,
        4 * out_channels,
        lambda r: jnp.where(
            r % rows < 4 * own_rows,
            r % rows // own_rows * out_channels + r // rows * own_rows + r % own_rows,
            -1,
        ),
    )
    packed = jnp.dot(
        order, grad_ref[...], precision=lax.Precision.HIGHEST, preferred_element_type=F32
    )
    pack_ref[...] = packed.reshape(count, rows, taps)


VM = pl.BlockSpec(memory_space=pltpu.VMEM)
SM = pl.BlockSpec(memory_space=pltpu.SMEM)


def call(kernel, outs, ins, scratch, flops, args, collective=None):
    extra = {} if collective is None else {"collective_id": collective, "has_side_effects": True}
    return pl.pallas_call(
        kernel,
        out_shape=outs,
        in_specs=ins,
        out_specs=jax.tree.map(lambda _: VM, outs),
        scratch_shapes=scratch,
        cost_estimate=pl.CostEstimate(flops=flops, bytes_accessed=1 << 22, transcendentals=0),
        compiler_params=pltpu.CompilerParams(vmem_limit_bytes=48 * 1024 * 1024, **extra),
    )(*args)


def per_device(features, labels, crop_block, weight, gain, shift, head, run_mean, run_var):
    slab = features[0]
    channels, planes, height, columns = slab.shape
    own_rows = weight.shape[0]
    devices = lax.axis_size("dev")
    roles = lax.axis_size("role")
    own_index = lax.axis_index("dev")
    out_channels = own_rows * devices
    taps = 9 * channels
    blocks = height // CY
    cell_rows = planes * CY
    cells = cell_rows * columns
    table = crop_block[0]
    slots = table.shape[1]
    dims = (planes, blocks, channels, out_channels, columns, slots)
    rows = -(-4 * own_rows // 16) * 16

    own_weight = weight.reshape(own_rows, 9, 3, channels).transpose(2, 0, 1, 3)
    own_weight = own_weight.reshape(3 * own_rows, taps)
    own_weight = jnp.pad(own_weight, ((0, rows - 3 * own_rows), (0, 0)))
    turned = jnp.pad(slab.transpose(1, 2, 0, 3), ((0, 0), (1, 1), (0, 0), (0, 0)))
    turned = turned.reshape(planes, (height + 2) * channels, columns)
    route = lax.dynamic_slice_in_dim(table, own_index, 1, 0)[0]
    live = (table >= 0).astype(F32)
    count = jnp.sum(live, 0) * cells
    counts = jnp.broadcast_to(count[:, None], (slots, LANES))
    live_wide = jnp.broadcast_to(live[:, :, None], live.shape + (LANES,))
    targets = labels[0].reshape(planes, blocks, CY, columns).transpose(1, 0, 2, 3)
    targets = targets.reshape(blocks, cell_rows, columns).astype(F32)

    shape = jax.ShapeDtypeStruct
    conv_flops = 2 * 27 * channels * out_channels * planes * height * columns
    patch = pltpu.VMEM((taps, cells), BF16)
    score_patch = pltpu.VMEM((taps, 8 * columns), BF16)
    tile = pltpu.VMEM((LANES, LANES), F32)
    small = pltpu.VMEM((slots, LANES), F32)
    held = pltpu.VMEM((devices, slots, LANES), F32)
    plane = pltpu.VMEM(turned.shape[1:], BF16)
    signals = pltpu.SemaphoreType.DMA((devices,))
    pair = pltpu.SemaphoreType.DMA((2,))
    params, u, norms, high, scores = call(
        functools.partial(forward_kernel, dims, devices, own_rows),
        (
            shape((4 * out_channels, taps), BF16),
            shape((blocks, out_channels, cells), BF16),
            shape((LANES, LANES), F32),
            shape(turned.shape[1:], BF16),
            shape((planes - 1, height, columns), F32),
        ),
        [SM] * 6 + [VM] * 4,
        [patch, tile, tile, pltpu.VMEM((rows, taps), BF16)]
        + [pltpu.VMEM((devices, rows, taps), BF16), small, held, plane, plane]
        + [signals] * 4
        + [pair] * 2,
        conv_flops * 2,
        (route, gain, shift, head, run_mean, run_var, own_weight, turned, live_wide, counts),
        0,
    )
    sums, vector_terms = call(
        functools.partial(sums_kernel, dims),
        (shape((slots, LANES), F32), shape((out_channels, columns), F32)),
        [SM, SM, VM, VM, VM, VM],
        [tile, tile],
        conv_flops // 16,
        (route, count, params, u, targets, norms),
    )
    means, last_scores = call(
        functools.partial(means_kernel, dims, devices),
        (shape((LANES, LANES), F32), shape((height, columns), F32)),
        [VM] * 5,
        [score_patch, tile, held, signals, signals],
        conv_flops,
        (params, turned, high, sums, counts),
        1,
    )
    packed = call(
        functools.partial(grad_kernel, dims),
        shape((devices, rows, taps), F32),
        [SM, SM] + [VM] * 7,
        [patch, pltpu.VMEM((3 * out_channels, cells), BF16)]
        + [pltpu.VMEM((4 * out_channels, taps), F32)],
        conv_flops,
        (route, count, params, turned, u, targets, norms, means, vector_terms),
    )
    part = pltpu.VMEM((rows, taps), F32)
    role_signals = pltpu.SemaphoreType.DMA((roles,))
    total = call(
        functools.partial(scatter_kernel, devices, roles),
        shape((rows, taps), F32),
        [VM],
        [pltpu.VMEM((devices, rows, taps), F32), part, pltpu.VMEM((roles, rows, taps), F32)]
        + [signals, signals, role_signals, role_signals],
        conv_flops // 16,
        (packed,),
        2,
    )
    weight_grad = total[: 3 * own_rows].reshape(3, own_rows, 9, channels).transpose(1, 2, 0, 3)
    weight_grad = weight_grad.reshape(own_rows, 27 * channels)
    vector_grad = total[3 * own_rows : 4 * own_rows, :3]
    return jnp.concatenate([scores, last_scores[None]], 0)[None], weight_grad, vector_grad


def solution(mesh):
    in_specs = (
        P("role", None, "dev", None, None),
        P("role", "dev", None, None),
        P("role", None, None),
        P("dev", None),
        P("dev"),
        P("dev"),
        P("dev"),
        P("dev"),
        P("dev"),
    )
    out_specs = (P("role", "dev", None, None), P("dev", None), P("dev", None))
    return jax.shard_map(
        per_device, mesh=mesh, in_specs=in_specs, out_specs=out_specs, check_vma=False
    )
```

time: 113 us -> 72.1 us (0.64)
  the two profiles are of different devices: /device:TPU:21 before, /device:TPU:0 now
where the time goes in v2:
time: 72.1 us; the launch traced here: 71.2 us
  Pallas kernels  64.4 us (89%)
  local copies, waits for them, and re-layouts  4.66 us (6%)
  other arithmetic  1.36 us (2%)
  between operations  0.8 us (1%)
    pallas_call x5, Pallas kernels, call(): pl.pallas_call(kernel, out_shape=outs, in_specs=ins, out_specs=jax.tree.m...  64.4 us
    unnamed x15, local copies, waits for them, and re-layouts  2 us

profile of v2, /device:TPU:0, one launch (start us, length us, event | category | flops | bytes accessed | tf_op | source)
XLA Modules:
  0.0 71.2 jit_solution(4028373109153296342)
XLA Ops:
  0.6 0.7 dynamic-slice_bitcast_fusion.route_ref
  1.3 0.7 %convert_reduce_fusion = (f32[16]{0:T(128)S(1)}, pred[1,16,16]{2,1,0:T(8,128)(4,1)S(1)}) fusion(s32[1,16,16]{2,1,0:T(8,128)} %param.11), kind=kLoop, calls=%fused_computation.1 | loop fusion | flops 752 | bytes 1344 | tf_op jit(solution)/shard_map/reduce_sum | solution.py:569
  2.1 0.1 broadcast_in_dim.9.counts_ref
  2.1 0.0 copy-start.6
  2.1 0.0 copy-start
  2.1 0.0 copy-start.1
  2.1 0.0 copy-start.2
  2.1 0.0 copy-start.3
  2.1 0.0 copy-start.4
  2.2 2.0 %copy.20 = bf16[2,64,32,128]{3,2,1,0:T(8,128)(2,1)S(1)} copy(bf16[2,64,32,128]{3,1,0,2:T(8,128)(2,1)} %bitcast.28) | data formatting | bytes 2097152
  4.1 0.2 pad.9.clone
  4.3 0.1 broadcast_in_dim.8.live_ref
  4.4 0.0 copy-done.6
  4.4 0.1 reshape.40
  4.6 0.1 reshape.41
  4.7 0.0 copy-done
  4.7 0.0 copy-done.1
  4.7 0.0 copy-done.2
  4.7 0.0 copy-done.3
  4.7 0.0 copy-done.4
  4.7 0.0 copy-start.5
  4.7 29.2 %shard_map.112 = (bf16[256,288]{1,0:T(8,128)(2,1)S(1)}, bf16[16,64,1024]{2,1,0:T(8,128)(2,1)S(1)}, f32[128,128]{1,0:T(8,128)S(1)}, bf16[2112,128]{1,0:T(8,128)(2,1)S(1)}, f32[1,64,128]{2,1,0:T(8,128)S(1)}) custom-call(s32[16]{0:T(128)S(1)} %dynamic-slice_bitcast_fusion.route_ref, f32[4]{0:T(128)S(1)} %copy-done, f32[4]{0:T(128)S(1)} %copy-done.1, ...), custom_call_target="tpu_custom_call" | custom-call | flops 3623878656 | bytes 4194304 | tf_op jit(solution)/shard_map/pallas_call | solution.py:534
  33.9 0.0 copy-done.5
  33.9 3.2 %shard_map.113 = (f32[16,128]{1,0:T(8,128)S(1)}, f32[64,128]{1,0:T(8,128)S(1)}) custom-call(s32[16]{0:T(128)S(1)} %dynamic-slice_bitcast_fusion.route_ref, f32[16]{0:T(128)S(1)} %broadcast_multiply_fusion.count_ref, bf16[256,288]{1,0:T(8,128)(2,1)S(1)} %get-tuple-element.13.param_ref, bf16[16,64,1024]{2,1,0:T(8,128)(2,1)S(1)} %get-tuple-element.15.u_ref, ...), custom_call_target="tpu_custom_call" | custom-call | flops 113246208 | bytes 4194304 | tf_op jit(solution)/shard_map/pallas_call | solution.py:534
  37.1 8.5 %shard_map.114 = (f32[128,128]{1,0:T(8,128)S(1)}, f32[64,128]{1,0:T(8,128)S(1)}) custom-call(bf16[256,288]{1,0:T(8,128)(2,1)S(1)} %get-tuple-element.13.param_ref, bf16[2,2112,128]{2,1,0:T(8,128)(2,1)S(1)} %bitcast.22, bf16[2112,128]{1,0:T(8,128)(2,1)S(1)} %get-tuple-element.14.high_ref, f32[16,128]{1,0:T(8,128)S(1)} %get-tuple-element.17.sum_ref, ...), custom_call_target="tpu_custom_call" | custom-call | flops 1811939328 | bytes 4194304 | tf_op jit(solution)/shard_map/pallas_call | solution.py:534
  45.6 6.3 %shard_map.115.chunk_ref = f32[16,16,288]{2,1,0:T(8,128)S(1)} custom-call(s32[16]{0:T(128)S(1)} %dynamic-slice_bitcast_fusion.route_ref, f32[16]{0:T(128)S(1)} %broadcast_multiply_fusion.count_ref, bf16[256,288]{1,0:T(8,128)(2,1)S(1)} %get-tuple-element.13.param_ref, bf16[2,2112,128]{2,1,0:T(8,128)(2,1)S(1)} %bitcast.23, ...), custom_call_target="tpu_custom_call" | custom-call | flops 1811939328 | bytes 4194304 | tf_op jit(solution)/shard_map/pallas_call | solution.py:534
  51.9 17.3 %shard_map.116 = f32[16,288]{1,0:T(8,128)S(1)} custom-call(f32[16,16,288]{2,1,0:T(8,128)S(1)} %shard_map.115.chunk_ref), custom_call_target="tpu_custom_call" | custom-call | flops 113246208 | bytes 4194304 | tf_op jit(solution)/shard_map/pallas_call | solution.py:534
  69.2 0.1 reshape.43
  69.3 0.7 reshape.44
  70.0 0.6 slice.7
  70.6 0.6 maximum_bitcast_fusion
  (6 shorter events, 0.1 us)
Async XLA Ops:
  2.1 2.3 %copy-start.6 = (f32[4,864]{1,0:T(4,128)S(1)}, f32[4,864]{1,0:T(4,128)}, u32[]{:S(2)}) copy-start(f32[4,864]{1,0:T(4,128)} %param.12) | copy-start | bytes 41476
  2.1 2.5 %copy-start = (f32[4]{0:T(128)S(1)}, f32[4]{0:T(128)}, u32[]{:S(2)}) copy-start(f32[4]{0:T(128)} %gain_ref.1) | copy-start | bytes 52
  2.1 2.5 %copy-start.1 = (f32[4]{0:T(128)S(1)}, f32[4]{0:T(128)}, u32[]{:S(2)}) copy-start(f32[4]{0:T(128)} %shift_ref.1) | copy-start | bytes 52
  2.1 2.5 %copy-start.2 = (f32[4]{0:T(128)S(1)}, f32[4]{0:T(128)}, u32[]{:S(2)}) copy-start(f32[4]{0:T(128)} %head_ref.1) | copy-start | bytes 52
  2.1 2.5 %copy-start.3 = (f32[4]{0:T(128)S(1)}, f32[4]{0:T(128)}, u32[]{:S(2)}) copy-start(f32[4]{0:T(128)} %mean_ref.1) | copy-start | bytes 52
  2.1 2.5 %copy-start.4 = (f32[4]{0:T(128)S(1)}, f32[4]{0:T(128)}, u32[]{:S(2)}) copy-start(f32[4]{0:T(128)} %spread_ref.1) | copy-start | bytes 52
  4.7 29.2 %copy-start.5 = (bf16[1,2,64,128]{3,2,1,0:T(8,128)(2,1)S(1)}, bf16[1,2,64,128]{3,2,1,0:T(8,128)(2,1)}, u32[]{:S(2)}) copy-start(bf16[1,2,64,128]{3,2,1,0:T(8,128)(2,1)} %param.10) | copy-start | bytes 98308

commit v3 on v2

--- a/solution.py
+++ b/solution.py
@@ -123,7 +123,7 @@
 
 
 def one_hot(rows, columns, target):
-    row = lax.broadcasted_iota(jnp.int32, (rows, columns), 0)
+    row = lax.broadcasted_iota(jnp.int32, (rows, 1), 0)
     return (lax.broadcasted_iota(jnp.int32, (rows, columns), 1) == target(row)).astype(F32)
 
 
@@ -224,14 +224,6 @@
             device_id_type=pl.DeviceIdType.MESH,
         )
 
-    @pl.when(me < count - 1)
-    def _():
-        halo(0).start()
-
-    @pl.when(me > 0)
-    def _():
-        halo(1).start()
-
     @pl.when(me == 0)
     def _():
         low[...] = jnp.zeros_like(low)
@@ -251,6 +243,15 @@
         + r % own_rows,
     ).astype(BF16)
     wait_all(*exchange)
+
+    @pl.when(me < count - 1)
+    def _():
+        halo(0).start()
+
+    @pl.when(me > 0)
+    def _():
+        halo(1).start()
+
     param_ref[...] = jnp.dot(
         order, held[...].reshape(count * rows, -1), preferred_element_type=F32
     ).astype(BF16)
@@ -357,16 +358,61 @@
 
 
 def scatter_kernel(
-    count, roles, chunk_ref, out_ref, held, part, others, sends, receives, role_sends, role_receives
+    count,
+    roles,
+    chunk_ref,
+    out_ref,
+    near,
+    mine,
+    held,
+    part,
+    others,
+    pair_sends,
+    pair_receives,
+    sends,
+    receives,
+    role_sends,
+    role_receives,
 ):
     me = lax.axis_index("dev")
+    side, chip, chips = lax.rem(me, 2), lax.div(me, 2), count // 2
     greet((("dev", count), ("role", roles)))
-    exchange = ("dev", count, lambda peer: chunk_ref.at[peer], held, sends, receives)
-    start_all(*exchange)
-    held[me] = chunk_ref[me]
-    wait_all(*exchange)
+    swap = pltpu.make_async_remote_copy(
+        src_ref=chunk_ref.at[1 - side],
+        dst_ref=near,
+        send_sem=pair_sends.at[0],
+        recv_sem=pair_receives.at[0],
+        device_id={"dev": me + 1 - 2 * side},
+        device_id_type=pl.DeviceIdType.MESH,
+    )
+    swap.start()
+    swap.wait()
+    mine[...] = chunk_ref[side] + near[...]
+
+    def to_chip(step):
+        peer = lax.rem(chip + step, chips)
+        return pltpu.make_async_remote_copy(
+            src_ref=mine.at[peer],
+            dst_ref=held.at[chip],
+            send_sem=sends.at[step],
+            recv_sem=receives.at[step],
+            device_id={"dev": peer * 2 + side},
+            device_id_type=pl.DeviceIdType.MESH,
+        )
+
+    def start(step, carry):
+        to_chip(step).start()
+        return carry
+
+    def wait(step, carry):
+        to_chip(step).wait()
+        return carry
+
+    lax.fori_loop(1, chips, start, 0)
+    held[chip] = mine[chip]
+    lax.fori_loop(1, chips, wait, 0)
     total = held[0]
-    for s in range(1, count):
+    for s in range(1, chips):
         total = total + held[s]
     part[...] = total
     exchange = ("role", roles, lambda peer: part, others, role_sends, role_receives)
@@ -470,11 +516,13 @@
     patch,
     field,
     grad_ref,
+    tail_ref,
 ):
     planes, blocks, channels, out_channels, columns, slots = dims
     cell_rows = planes * CY
-    count, rows, taps = pack_ref.shape
+    count = 2 * pack_ref.shape[1]
     own_rows = out_channels // count
+    taps = 9 * channels
     patch[...] = jnp.zeros_like(patch)
     grad_ref[...] = jnp.zeros_like(grad_ref)
 
@@ -502,27 +550,34 @@
                 field[0:out_channels, where] = shift_lanes(du, 1).astype(BF16)
                 field[out_channels : 2 * out_channels, where] = du.astype(BF16)
                 field[2 * out_channels :, where] = shift_lanes(du, -1).astype(BF16)
-            grad_ref[0 : 3 * out_channels, :] += lax.dot_general(
+            grad_ref[:, 0:taps] += lax.dot_general(
                 field[...], patch[...], (((1,), (1,)), ((), ())), preferred_element_type=F32
             )
 
         return carry
 
     lax.fori_loop(0, slots, step, 0)
-    grad_ref[3 * out_channels :, 0:LANES] = vec_ref[...]
-    order = one_hot(
-        count * rows,
-        4 * out_channels,
-        lambda r: jnp.where(
-            r % rows < 4 * own_rows,
-            r % rows // own_rows * out_channels + r // rows * own_rows + r % own_rows,
-            -1,
-        ),
-    )
-    packed = jnp.dot(
-        order, grad_ref[...], precision=lax.Precision.HIGHEST, preferred_element_type=F32
-    )
-    pack_ref[...] = packed.reshape(count, rows, taps)
+    full = taps // LANES
+    rest = taps - full * LANES
+    tail = pltpu.roll(vec_ref[...], 3 * rest, 1)
+    for tap in range(3):
+        part = grad_ref[tap * out_channels : (tap + 1) * out_channels, full * LANES :]
+        tail = tail + (pltpu.roll(part, tap * rest, 1) if tap else part)
+    tail_ref[...] = tail
+    pack_ref[...] = jnp.zeros_like(pack_ref)
+    for owner in range(count):
+        own = owner * own_rows
+        for group in range(full):
+            for tap in range(3):
+                start = (group * 3 + tap) * own_rows
+                row = tap * out_channels + own
+                pack_ref[owner % 2, owner // 2, start : start + own_rows, :] = grad_ref[
+                    row : row + own_rows, group * LANES : (group + 1) * LANES
+                ]
+        start = 3 * full * own_rows
+        pack_ref[owner % 2, owner // 2, start : start + own_rows, :] = tail_ref[
+            own : own + own_rows, :
+        ]
 
 
 VM = pl.BlockSpec(memory_space=pltpu.VMEM)
@@ -617,30 +672,42 @@
         (params, turned, high, sums, counts),
         1,
     )
+    full = taps // LANES
+    rest = taps - full * LANES
+    pack_rows = -(-(3 * full + 1) * own_rows // 8) * 8
+    chips = devices // 2
     packed = call(
         functools.partial(grad_kernel, dims),
-        shape((devices, rows, taps), F32),
+        shape((2, chips, pack_rows, LANES), F32),
         [SM, SM] + [VM] * 7,
         [patch, pltpu.VMEM((3 * out_channels, cells), BF16)]
-        + [pltpu.VMEM((4 * out_channels, taps), F32)],
+        + [pltpu.VMEM((3 * out_channels, (full + 1) * LANES), F32)]
+        + [pltpu.VMEM((out_channels, LANES), F32)],
         conv_flops,
         (route, count, params, turned, u, targets, norms, means, vector_terms),
     )
-    part = pltpu.VMEM((rows, taps), F32)
+    chunks = pltpu.VMEM((chips, pack_rows, LANES), F32)
+    part = pltpu.VMEM((pack_rows, LANES), F32)
     role_signals = pltpu.SemaphoreType.DMA((roles,))
+    chip_signals = pltpu.SemaphoreType.DMA((chips,))
     total = call(
         functools.partial(scatter_kernel, devices, roles),
-        shape((rows, taps), F32),
+        shape((pack_rows, LANES), F32),
         [VM],
-        [pltpu.VMEM((devices, rows, taps), F32), part, pltpu.VMEM((roles, rows, taps), F32)]
-        + [signals, signals, role_signals, role_signals],
+        [chunks, chunks, chunks, part, pltpu.VMEM((roles, pack_rows, LANES), F32)]
+        + [pair, pair, chip_signals, chip_signals, role_signals, role_signals],
         conv_flops // 16,
         (packed,),
         2,
     )
-    weight_grad = total[: 3 * own_rows].reshape(3, own_rows, 9, channels).transpose(1, 2, 0, 3)
+    split = 3 * full * own_rows
+    front = total[:split].reshape(full, 3, own_rows, LANES).transpose(1, 2, 0, 3)
+    back = total[split : split + own_rows]
+    sides = back[:, : 3 * rest].reshape(own_rows, 3, rest).transpose(1, 0, 2)
+    weight_grad = jnp.concatenate([front.reshape(3, own_rows, full * LANES), sides], 2)
+    weight_grad = weight_grad.reshape(3, own_rows, 9, channels).transpose(1, 2, 0, 3)
     weight_grad = weight_grad.reshape(own_rows, 27 * channels)
-    vector_grad = total[3 * own_rows : 4 * own_rows, :3]
+    vector_grad = back[:, 3 * rest : 3 * rest + 3]
     return jnp.concatenate([scores, last_scores[None]], 0)[None], weight_grad, vector_grad
 
 

time: 72.1 us -> 70.8 us (0.982); the launches traced: 71.2 us -> 71.5 us
  no operation moved by 1% of the time
where the time goes in v3:
time: 70.8 us; the launch traced here: 71.5 us
  Pallas kernels  64.4 us (91%)
  local copies, waits for them, and re-layouts  4.83 us (7%)
  other arithmetic  1.37 us (2%)
  between operations  0.83 us (1%)
    pallas_call x5, Pallas kernels, call(): pl.pallas_call(kernel, out_shape=outs, in_specs=ins, out_specs=jax.tree.m...  64.4 us
    unnamed x15, local copies, waits for them, and re-layouts  2 us

profile of v3, /device:TPU:0, one launch (start us, length us, event | category | flops | bytes accessed | tf_op | source)
XLA Modules:
  0.0 71.5 jit_solution(15562956086696225377)
XLA Ops:
  0.6 0.7 dynamic-slice_bitcast_fusion.route_ref
  1.3 0.7 convert_reduce_fusion
  2.1 0.1 broadcast_in_dim.9.counts_ref
  2.1 0.0 copy-start.6
  2.1 0.0 copy-start
  2.1 0.0 copy-start.1
  2.1 0.0 copy-start.2
  2.1 0.0 copy-start.3
  2.1 0.0 copy-start.4
  2.2 2.0 %copy.22 = bf16[2,64,32,128]{3,2,1,0:T(8,128)(2,1)S(1)} copy(bf16[2,64,32,128]{3,1,0,2:T(8,128)(2,1)} %bitcast.35) | data formatting | bytes 2097152
  4.1 0.2 pad.9.clone
  4.3 0.1 broadcast_in_dim.8.live_ref
  4.4 0.0 copy-done.6
  4.4 0.1 reshape.49
  4.6 0.1 reshape.50
  4.7 0.0 copy-done
  4.7 0.0 copy-done.1
  4.7 0.0 copy-done.2
  4.7 0.0 copy-done.3
  4.7 0.0 copy-done.4
  4.7 0.0 copy-start.5
  4.7 29.0 %shard_map.112 = (bf16[256,288]{1,0:T(8,128)(2,1)S(1)}, bf16[16,64,1024]{2,1,0:T(8,128)(2,1)S(1)}, f32[128,128]{1,0:T(8,128)S(1)}, bf16[2112,128]{1,0:T(8,128)(2,1)S(1)}, f32[1,64,128]{2,1,0:T(8,128)S(1)}) custom-call(s32[16]{0:T(128)S(1)} %dynamic-slice_bitcast_fusion.route_ref, f32[4]{0:T(128)S(1)} %copy-done, f32[4]{0:T(128)S(1)} %copy-done.1, ...), custom_call_target="tpu_custom_call" | custom-call | flops 3623878656 | bytes 4194304 | tf_op jit(solution)/shard_map/pallas_call | solution.py:589
  33.8 0.0 copy-done.5
  33.8 3.5 %shard_map.113 = (f32[16,128]{1,0:T(8,128)S(1)}, f32[64,128]{1,0:T(8,128)S(1)}) custom-call(s32[16]{0:T(128)S(1)} %dynamic-slice_bitcast_fusion.route_ref, f32[16]{0:T(128)S(1)} %broadcast_multiply_fusion.count_ref, bf16[256,288]{1,0:T(8,128)(2,1)S(1)} %get-tuple-element.13.param_ref, bf16[16,64,1024]{2,1,0:T(8,128)(2,1)S(1)} %get-tuple-element.15.u_ref, ...), custom_call_target="tpu_custom_call" | custom-call | flops 113246208 | bytes 4194304 | tf_op jit(solution)/shard_map/pallas_call | solution.py:589
  37.3 9.5 %shard_map.114 = (f32[128,128]{1,0:T(8,128)S(1)}, f32[64,128]{1,0:T(8,128)S(1)}) custom-call(bf16[256,288]{1,0:T(8,128)(2,1)S(1)} %get-tuple-element.13.param_ref, bf16[2,2112,128]{2,1,0:T(8,128)(2,1)S(1)} %bitcast.30, bf16[2112,128]{1,0:T(8,128)(2,1)S(1)} %get-tuple-element.14.high_ref, f32[16,128]{1,0:T(8,128)S(1)} %get-tuple-element.17.sum_ref, ...), custom_call_target="tpu_custom_call" | custom-call | flops 1811939328 | bytes 4194304 | tf_op jit(solution)/shard_map/pallas_call | solution.py:589
  46.8 6.4 %shard_map.115.chunk_ref = f32[2,8,32,128]{3,2,1,0:T(8,128)S(1)} custom-call(s32[16]{0:T(128)S(1)} %dynamic-slice_bitcast_fusion.route_ref, f32[16]{0:T(128)S(1)} %broadcast_multiply_fusion.count_ref, bf16[256,288]{1,0:T(8,128)(2,1)S(1)} %get-tuple-element.13.param_ref, bf16[2,2112,128]{2,1,0:T(8,128)(2,1)S(1)} %bitcast.31, ...), custom_call_target="tpu_custom_call" | custom-call | flops 1811939328 | bytes 4194304 | tf_op jit(solution)/shard_map/pallas_call | solution.py:589
  53.2 16.0 %shard_map.116 = f32[32,128]{1,0:T(8,128)S(1)} custom-call(f32[2,8,32,128]{3,2,1,0:T(8,128)S(1)} %shard_map.115.chunk_ref), custom_call_target="tpu_custom_call" | custom-call | flops 113246208 | bytes 4194304 | tf_op jit(solution)/shard_map/pallas_call | solution.py:589
  69.2 0.1 reshape.54
  69.3 0.1 reshape.55
  69.5 0.7 reshape.56
  70.2 0.6 slice.14
  70.8 0.6 maximum_bitcast_fusion
  (11 shorter events, 0.1 us)
Async XLA Ops:
  2.1 2.3 %copy-start.6 = (f32[4,864]{1,0:T(4,128)S(1)}, f32[4,864]{1,0:T(4,128)}, u32[]{:S(2)}) copy-start(f32[4,864]{1,0:T(4,128)} %param.12) | copy-start | bytes 41476
  2.1 2.5 %copy-start = (f32[4]{0:T(128)S(1)}, f32[4]{0:T(128)}, u32[]{:S(2)}) copy-start(f32[4]{0:T(128)} %gain_ref.1) | copy-start | bytes 52
  2.1 2.5 %copy-start.1 = (f32[4]{0:T(128)S(1)}, f32[4]{0:T(128)}, u32[]{:S(2)}) copy-start(f32[4]{0:T(128)} %shift_ref.1) | copy-start | bytes 52
  2.1 2.5 %copy-start.2 = (f32[4]{0:T(128)S(1)}, f32[4]{0:T(128)}, u32[]{:S(2)}) copy-start(f32[4]{0:T(128)} %head_ref.1) | copy-start | bytes 52
  2.1 2.5 %copy-start.3 = (f32[4]{0:T(128)S(1)}, f32[4]{0:T(128)}, u32[]{:S(2)}) copy-start(f32[4]{0:T(128)} %mean_ref.1) | copy-start | bytes 52
  2.1 2.5 %copy-start.4 = (f32[4]{0:T(128)S(1)}, f32[4]{0:T(128)}, u32[]{:S(2)}) copy-start(f32[4]{0:T(128)} %spread_ref.1) | copy-start | bytes 52
  4.7 29.1 %copy-start.5 = (bf16[1,2,64,128]{3,2,1,0:T(8,128)(2,1)S(1)}, bf16[1,2,64,128]{3,2,1,0:T(8,128)(2,1)}, u32[]{:S(2)}) copy-start(bf16[1,2,64,128]{3,2,1,0:T(8,128)(2,1)} %param.10) | copy-start | bytes 98308

commit v4 on v3

--- a/solution.py
+++ b/solution.py
@@ -224,6 +224,14 @@
             device_id_type=pl.DeviceIdType.MESH,
         )
 
+    @pl.when(me < count - 1)
+    def _():
+        halo(0).start()
+
+    @pl.when(me > 0)
+    def _():
+        halo(1).start()
+
     @pl.when(me == 0)
     def _():
         low[...] = jnp.zeros_like(low)
@@ -243,14 +251,6 @@
         + r % own_rows,
     ).astype(BF16)
     wait_all(*exchange)
-
-    @pl.when(me < count - 1)
-    def _():
-        halo(0).start()
-
-    @pl.when(me > 0)
-    def _():
-        halo(1).start()
 
     param_ref[...] = jnp.dot(
         order, held[...].reshape(count * rows, -1), preferred_element_type=F32
@@ -376,7 +376,19 @@
 ):
     me = lax.axis_index("dev")
     side, chip, chips = lax.rem(me, 2), lax.div(me, 2), count // 2
-    greet((("dev", count), ("role", roles)))
+    barrier = pltpu.get_barrier_semaphore()
+
+    def tell(**where):
+        pl.semaphore_signal(
+            barrier, inc=1, device_id=where, device_id_type=pl.DeviceIdType.MESH
+        )
+
+    tell(dev=me + 1 - 2 * side)
+    for step in range(1, chips):
+        tell(dev=lax.rem(chip + step, chips) * 2 + side)
+    for step in range(1, roles):
+        tell(role=lax.rem(lax.axis_index("role") + step, roles))
+    pl.semaphore_wait(barrier, chips + roles - 1)
     swap = pltpu.make_async_remote_copy(
         src_ref=chunk_ref.at[1 - side],
         dst_ref=near,

time: 70.8 us -> 68.6 us (0.969); the launches traced: 71.5 us -> 68 us
  Pallas kernels: 64.4 us -> 61 us
    pallas_call x5, Pallas kernels: 64.4 us -> 61 us  [call(): pl.pallas_call(kernel, out_shape=outs, in_specs=ins, out_specs=jax.tree.m...]
where the time goes in v4:
time: 68.6 us; the launch traced here: 68 us
  Pallas kernels  61 us (89%)
  local copies, waits for them, and re-layouts  4.83 us (7%)
  other arithmetic  1.37 us (2%)
  between operations  0.83 us (1%)
    pallas_call x5, Pallas kernels, call(): pl.pallas_call(kernel, out_shape=outs, in_specs=ins, out_specs=jax.tree.m...  61 us
    unnamed x15, local copies, waits for them, and re-layouts  2 us

profile of v4, /device:TPU:0, one launch (start us, length us, event | category | flops | bytes accessed | tf_op | source)
XLA Modules:
  0.0 68.0 jit_solution(14214277132243736736)
XLA Ops:
  0.6 0.7 %dynamic-slice_bitcast_fusion.route_ref = s32[16]{0:T(128)S(1)} fusion(s32[1,16,16]{2,1,0:T(8,128)} %param.11, s32[]{:T(128)S(6)} %select_n.3), kind=kLoop, calls=%fused_computation.7 | loop fusion | bytes 132 | tf_op jit(solution)/shard_map/squeeze | solution.py:634
  1.3 0.7 %convert_reduce_fusion = (f32[16]{0:T(128)S(1)}, pred[1,16,16]{2,1,0:T(8,128)(4,1)S(1)}) fusion(s32[1,16,16]{2,1,0:T(8,128)} %param.11), kind=kLoop, calls=%fused_computation.3 | loop fusion | flops 752 | bytes 1344 | tf_op jit(solution)/shard_map/reduce_sum | solution.py:636
  2.1 0.1 broadcast_in_dim.9.counts_ref
  2.1 0.0 copy-start.6
  2.1 0.0 copy-start
  2.1 0.0 copy-start.1
  2.1 0.0 copy-start.2
  2.1 0.0 copy-start.3
  2.1 0.0 copy-start.4
  2.2 2.0 %copy.22 = bf16[2,64,32,128]{3,2,1,0:T(8,128)(2,1)S(1)} copy(bf16[2,64,32,128]{3,1,0,2:T(8,128)(2,1)} %bitcast.35) | data formatting | bytes 2097152
  4.1 0.2 pad.9.clone
  4.3 0.1 broadcast_in_dim.8.live_ref
  4.4 0.0 copy-done.6
  4.4 0.1 reshape.49
  4.6 0.1 reshape.50
  4.7 0.0 copy-done
  4.7 0.0 copy-done.1
  4.7 0.0 copy-done.2
  4.7 0.0 copy-done.3
  4.7 0.0 copy-done.4
  4.7 0.0 copy-start.5
  4.7 29.2 %shard_map.112 = (bf16[256,288]{1,0:T(8,128)(2,1)S(1)}, bf16[16,64,1024]{2,1,0:T(8,128)(2,1)S(1)}, f32[128,128]{1,0:T(8,128)S(1)}, bf16[2112,128]{1,0:T(8,128)(2,1)S(1)}, f32[1,64,128]{2,1,0:T(8,128)S(1)}) custom-call(s32[16]{0:T(128)S(1)} %dynamic-slice_bitcast_fusion.route_ref, f32[4]{0:T(128)S(1)} %copy-done, f32[4]{0:T(128)S(1)} %copy-done.1, ...), custom_call_target="tpu_custom_call" | custom-call | flops 3623878656 | bytes 4194304 | tf_op jit(solution)/shard_map/pallas_call | solution.py:601
  33.9 0.0 copy-done.5
  33.9 3.2 %shard_map.113 = (f32[16,128]{1,0:T(8,128)S(1)}, f32[64,128]{1,0:T(8,128)S(1)}) custom-call(s32[16]{0:T(128)S(1)} %dynamic-slice_bitcast_fusion.route_ref, f32[16]{0:T(128)S(1)} %broadcast_multiply_fusion.count_ref, bf16[256,288]{1,0:T(8,128)(2,1)S(1)} %get-tuple-element.13.param_ref, bf16[16,64,1024]{2,1,0:T(8,128)(2,1)S(1)} %get-tuple-element.15.u_ref, ...), custom_call_target="tpu_custom_call" | custom-call | flops 113246208 | bytes 4194304 | tf_op jit(solution)/shard_map/pallas_call | solution.py:601
  37.1 8.2 %shard_map.114 = (f32[128,128]{1,0:T(8,128)S(1)}, f32[64,128]{1,0:T(8,128)S(1)}) custom-call(bf16[256,288]{1,0:T(8,128)(2,1)S(1)} %get-tuple-element.13.param_ref, bf16[2,2112,128]{2,1,0:T(8,128)(2,1)S(1)} %bitcast.30, bf16[2112,128]{1,0:T(8,128)(2,1)S(1)} %get-tuple-element.14.high_ref, f32[16,128]{1,0:T(8,128)S(1)} %get-tuple-element.17.sum_ref, ...), custom_call_target="tpu_custom_call" | custom-call | flops 1811939328 | bytes 4194304 | tf_op jit(solution)/shard_map/pallas_call | solution.py:601
  45.3 5.7 %shard_map.115.chunk_ref = f32[2,8,32,128]{3,2,1,0:T(8,128)S(1)} custom-call(s32[16]{0:T(128)S(1)} %dynamic-slice_bitcast_fusion.route_ref, f32[16]{0:T(128)S(1)} %broadcast_multiply_fusion.count_ref, bf16[256,288]{1,0:T(8,128)(2,1)S(1)} %get-tuple-element.13.param_ref, bf16[2,2112,128]{2,1,0:T(8,128)(2,1)S(1)} %bitcast.31, ...), custom_call_target="tpu_custom_call" | custom-call | flops 1811939328 | bytes 4194304 | tf_op jit(solution)/shard_map/pallas_call | solution.py:601
  51.1 14.7 %shard_map.116 = f32[32,128]{1,0:T(8,128)S(1)} custom-call(f32[2,8,32,128]{3,2,1,0:T(8,128)S(1)} %shard_map.115.chunk_ref), custom_call_target="tpu_custom_call" | custom-call | flops 113246208 | bytes 4194304 | tf_op jit(solution)/shard_map/pallas_call | solution.py:601
  65.8 0.1 reshape.54
  65.9 0.1 reshape.55
  66.1 0.7 %reshape.56 = f32[4,864]{1,0:T(4,128)} reshape(f32[4,9,3,32]{3,2,1,0:T(4,128)S(1)} %copy.21) | data formatting | bytes 27648 | tf_op jit(solution)/shard_map/reshape | solution.py:721
  66.8 0.6 slice.14
  67.4 0.6 maximum_bitcast_fusion
  (11 shorter events, 0.1 us)
Async XLA Ops:
  2.1 2.3 %copy-start.6 = (f32[4,864]{1,0:T(4,128)S(1)}, f32[4,864]{1,0:T(4,128)}, u32[]{:S(2)}) copy-start(f32[4,864]{1,0:T(4,128)} %param.12) | copy-start | bytes 41476
  2.1 2.5 %copy-start = (f32[4]{0:T(128)S(1)}, f32[4]{0:T(128)}, u32[]{:S(2)}) copy-start(f32[4]{0:T(128)} %gain_ref.1) | copy-start | bytes 52
  2.1 2.5 %copy-start.1 = (f32[4]{0:T(128)S(1)}, f32[4]{0:T(128)}, u32[]{:S(2)}) copy-start(f32[4]{0:T(128)} %shift_ref.1) | copy-start | bytes 52
  2.1 2.5 %copy-start.2 = (f32[4]{0:T(128)S(1)}, f32[4]{0:T(128)}, u32[]{:S(2)}) copy-start(f32[4]{0:T(128)} %head_ref.1) | copy-start | bytes 52
  2.1 2.5 %copy-start.3 = (f32[4]{0:T(128)S(1)}, f32[4]{0:T(128)}, u32[]{:S(2)}) copy-start(f32[4]{0:T(128)} %mean_ref.1) | copy-start | bytes 52
  2.1 2.5 %copy-start.4 = (f32[4]{0:T(128)S(1)}, f32[4]{0:T(128)}, u32[]{:S(2)}) copy-start(f32[4]{0:T(128)} %spread_ref.1) | copy-start | bytes 52
  4.7 29.2 %copy-start.5 = (bf16[1,2,64,128]{3,2,1,0:T(8,128)(2,1)S(1)}, bf16[1,2,64,128]{3,2,1,0:T(8,128)(2,1)}, u32[]{:S(2)}) copy-start(bf16[1,2,64,128]{3,2,1,0:T(8,128)(2,1)} %param.10) | copy-start | bytes 98308
